TPU v7x, 32 devices: a whole 2x2x4 slice. The times are simulated.
32 devices in a mesh: cent: 8 (over z, y), grp: 4 (over x, core).
Axes of the slice: x: 2, y: 2, z: 4, core: 2. Of those that a mesh axis runs over, the one named last changes fastest.
Arguments:
- queries: bfloat16 [64, 32, 128], P('grp'), may hold values from -6 to 6
- centroids: bfloat16 [262144, 128], P('cent'), may hold values from -0.5 to 0.5
- candidates: int32 [4, 8, 2, 64], P('grp', 'cent'), may hold values from 0 to 16383, as said below
- token_codes: int32 [16384, 128], P(('cent', 'grp')), may hold values from 0 to 32767
- resid_words: int32 [16384, 32, 128], P(('cent', 'grp')), may hold values from 0 to 255
- lengths: int32 [16384], P(('cent', 'grp')), may hold values from 1 to 128
- levels: float32 [4, 128], replicated, may hold values from -0.3125 to 0.3125
Outputs:
- token_best: float32 [64, 32], P('grp')
- passage_scores: float32 [4, 8, 2, 64], P('grp', 'cent')
Inputs may be any that keep to these rules, and one draw needn't show every extreme that they name: `candidates`: the entries of one [g, c] block are all different and name at most 8 passages of any one owner block (passages owner * 512 to owner * 512 + 511); one owner block gets exactly 8 from every [g, c] block.
All inputs are finite; a program needn't handle non-finite values.
Results may differ from a plain program's by a relative error of at most 0.0003.
Values may be sent and summed in bfloat16 or wider, within the bound.
No kernel may reach another device: no remote copies, remote signals or barrier semaphores. Data moves between devices by JAX's collectives and lax.ppermute only.
A program may use at most 128 MiB of HBM per device.

v0:
```python
import functools

import jax
import jax.numpy as jnp
from jax import lax
from jax.experimental import pallas as pl
from jax.experimental.pallas import tpu as pltpu
from jax.sharding import PartitionSpec as P

MASKED = -1000000000.0
LANES = 128
SUB = 8
FIELDS = 4
BLOCKS = 16
ALIGN = 8
SLOTS = 4
MIB = 1 << 20


def transposed_by_eye(row):
    size = row.shape[1]
    down = lax.broadcasted_iota(jnp.int32, (size, size), 0)
    across = lax.broadcasted_iota(jnp.int32, (size, size), 1)
    return jnp.sum(jnp.where(down == across, row, 0.0), axis=1, keepdims=True)


def one_row(rows):
    return jnp.concatenate([rows[index : index + 1, :] for index in range(rows.shape[0])], axis=1)


def slots_kernel(pass_dev, capacity, cand_ref, slots_ref, target_ref):
    per_device = cand_ref.shape[0]
    ids = one_row(cand_ref[...])
    pairs = ids.shape[1]
    owners = jnp.right_shift(ids, pass_dev.bit_length() - 1)
    earlier = lax.broadcasted_iota(jnp.int32, (pairs, pairs), 0) < lax.broadcasted_iota(
        jnp.int32, (pairs, pairs), 1
    )
    named = owners.astype(jnp.float32)
    same = transposed_by_eye(named) == named
    slots = jnp.sum(jnp.where(same & earlier, 1.0, 0.0), axis=0, keepdims=True).astype(jnp.int32)
    target_ref[...] = owners * capacity + slots
    query = lax.broadcasted_iota(jnp.int32, ids.shape, 1) // (pairs // per_device)
    tagged = (jnp.bitwise_and(ids, pass_dev - 1) * per_device + query + 1).astype(jnp.float32)
    down = lax.broadcasted_iota(jnp.int32, (slots_ref.shape[0], pairs), 0)
    lane = lax.broadcasted_iota(jnp.int32, slots_ref.shape, 1)
    found = jnp.zeros(slots_ref.shape, jnp.float32)
    for slot in range(capacity):
        chosen = jnp.where((down == owners) & (slots == slot), tagged, 0.0)
        found = jnp.where(lane == slot, jnp.sum(chosen, axis=1, keepdims=True), found)
    slots_ref[...] = found.astype(jnp.int32)


def slots_by_owner(cand, devices, pass_dev, capacity):
    vmem = pl.BlockSpec(memory_space=pltpu.VMEM)
    return pl.pallas_call(
        functools.partial(slots_kernel, pass_dev, capacity),
        in_specs=[vmem],
        out_specs=[vmem] * 2,
        out_shape=[
            jax.ShapeDtypeStruct((devices, capacity), jnp.int32),
            jax.ShapeDtypeStruct((1, cand.size), jnp.int32),
        ],
        name="slots_by_owner",
    )(cand)


def score_kernel(
    sizes,
    me_ref,
    ids,
    own_ref,
    levels_ref,
    cent_hbm,
    words_hbm,
    codes_hbm,
    lens_hbm,
    *rest,
):
    group_count, cent_count, per_device, query_len, capacity, pass_dev, cand_count = sizes
    query_hbm = rest[:group_count]
    (out_ref, staged, table, words, query_rows, query_t, own_t, dense, embed, maxima, codes, word_stage,
     code_stage, *more) = rest[group_count:]
    code_slots, more = more[:SLOTS], more[SLOTS:]
    (lens, work, work_quad, item_pass, item_len, item_lane, table_sem, words_sem, query_sem, small_sem,
     slot_sem) = more
    sources = ids.shape[0]
    items = sources * capacity
    tiles = words.shape[1] // SUB
    tile_tokens = SUB * FIELDS
    quad_sources = LANES // (per_device * query_len)
    quads = sources // quad_sources
    group_quads = cent_count // quad_sources
    per_bits = per_device.bit_length() - 1
    tile_bits = tiles.bit_length() - 1
    part_rows = staged.shape[0] // quads
    word_parts = words_sem.shape[0]
    part_pass = pass_dev // word_parts

    def table_copy(part):
        rows = pl.ds(pl.multiple_of(part * part_rows, part_rows), part_rows)
        return pltpu.make_async_copy(cent_hbm.at[rows, :], staged.at[rows, :], table_sem.at[part])

    def words_copy(part):
        rows = pl.ds(part * part_pass, part_pass)
        return pltpu.make_async_copy(words_hbm.at[rows], words.at[rows], words_sem.at[part])

    def start_table(part, carry):
        table_copy(part).start()
        return carry

    group = jnp.bitwise_and(me_ref[0], group_count - 1)

    def query_copy(apart):
        return pltpu.make_async_copy(
            query_hbm[apart], query_rows.at[jnp.bitwise_xor(group, apart)], query_sem.at[apart]
        )

    lens_copy = pltpu.make_async_copy(lens_hbm, lens, small_sem.at[0])
    codes_copy = pltpu.make_async_copy(codes_hbm, codes, small_sem.at[1])
    lens_copy.start()
    for apart in range(group_count):
        query_copy(apart).start()
    lax.fori_loop(0, quads, start_table, 0)
    codes_copy.start()
    for part in range(word_parts):
        words_copy(part).start()

    maxima[...] = jnp.full(maxima.shape, MASKED, jnp.float32)
    own_t[...] = jnp.transpose(own_ref[...].astype(jnp.float32)).astype(jnp.bfloat16)
    lens_copy.wait()
    for apart in range(group_count):
        query_copy(apart).wait()

    item_pass[items] = 0
    item_len[items] = 0
    item_lane[items] = -1
    spare = items * tiles

    def prepare(quad, carry):
        count, best = carry
        table_copy(quad).wait()
        rows = pl.ds(pl.multiple_of(quad * part_rows, part_rows), part_rows)
        scores = jnp.dot(staged[rows, :], own_t[...], preferred_element_type=jnp.float32)
        best = jnp.maximum(best, jnp.max(scores.reshape(part_rows // SUB, SUB, scores.shape[1]), axis=0))
        table[rows, :] = staged[rows, :].astype(jnp.float32)
        block = query_rows[quad // group_quads, pl.ds(quad % group_quads * LANES, LANES), :]
        query_t[quad] = jnp.transpose(block.astype(jnp.float32)).astype(jnp.bfloat16)
        start = count
        found = []
        for part in range(quad_sources):
            cent = quad % group_quads * quad_sources + part
            source = cent * group_count + quad // group_quads
            found += [(part, source * capacity + slot, ids[source, slot] - 1) for slot in range(capacity)]
        found = [(part, item, tag, jnp.maximum(tag, 0)) for part, item, tag in found]
        lengths = [lens[jnp.right_shift(held, per_bits)] for _, _, _, held in found]
        for (part, item, tag, held), length in zip(found, lengths):
            item_pass[item] = jnp.right_shift(held, per_bits)
            item_len[item] = length
            item_lane[item] = part * per_device + jnp.bitwise_and(held, per_device - 1)
            for tile in range(tiles):
                work[count + tile] = item * tiles + tile
            blocks = jnp.right_shift(length + tile_tokens - 1, tile_tokens.bit_length() - 1)
            count = count + jnp.where(tag >= 0, blocks, 0)
        for index in range(ALIGN):
            work[count + index] = spare
        count = (count + ALIGN - 1) // ALIGN * ALIGN
        for index in range(quad_sources * capacity * tiles // ALIGN):
            work_quad[start // ALIGN + index] = quad
        return count, best

    lowest = jnp.full((SUB, own_t.shape[1]), -jnp.inf, jnp.float32)
    total, token_best = lax.fori_loop(0, quads, prepare, (0, lowest))
    token_best = jnp.max(token_best, axis=0, keepdims=True)
    for index in range((SLOTS + 1) * BLOCKS):
        work[total + index] = spare
    for index in range(2 * BLOCKS // ALIGN):
        work_quad[total // ALIGN + index] = 0
    chunks = jnp.maximum((total + BLOCKS - 1) // BLOCKS, 2)
    codes_copy.wait()
    for part in range(word_parts):
        words_copy(part).wait()

    sub = lax.broadcasted_iota(jnp.int32, (SUB, LANES), 0)
    position = jnp.concatenate([sub * FIELDS + field for field in range(FIELDS)], axis=0)
    row_blocks = LANES // tile_tokens
    lane_tile = lax.broadcasted_iota(jnp.int32, (1, LANES), 1) // tile_tokens
    lane_group = lax.broadcasted_iota(jnp.int32, (1, LANES), 1) // query_len
    level = [levels_ref[index : index + 1, :] for index in range(FIELDS)]

    def score(chunk):
        scores = []
        for part in range(BLOCKS // ALIGN):
            rows = embed[part * ALIGN * tile_tokens : (part + 1) * ALIGN * tile_tokens, :]
            quad = work_quad[chunk * (BLOCKS // ALIGN) + part]
            scores.append(jnp.dot(rows, query_t[quad], preferred_element_type=jnp.float32))
        for index in range(BLOCKS):
            entry = work[chunk * BLOCKS + index]
            item, tile = jnp.right_shift(entry, tile_bits), jnp.bitwise_and(entry, tiles - 1)
            inner = index % ALIGN
            block = scores[index // ALIGN][inner * tile_tokens : (inner + 1) * tile_tokens]
            kept = jnp.where(position < item_len[item] - tile * tile_tokens, block, MASKED)
            best = jnp.max(kept, axis=0, keepdims=True)
            maxima[tile, pl.ds(item, 1), :] = jnp.where(lane_group == item_lane[item], best, 0.0)

    def slot_copy(slot):
        return pltpu.make_async_copy(code_stage.at[slot], code_slots[slot], slot_sem.at[slot])

    def fetch(chunk, slot):
        for row in range(BLOCKS // row_blocks):
            together = jnp.zeros((1, LANES), jnp.int32)
            for index in range(row_blocks):
                block = row * row_blocks + index
                entry = work[chunk * BLOCKS + block]
                passage = item_pass[jnp.right_shift(entry, tile_bits)]
                tile = jnp.bitwise_and(entry, tiles - 1)
                shift = jnp.bitwise_and(index - tile, row_blocks - 1) * tile_tokens
                moved = pltpu.roll(codes[pl.ds(passage, 1), :], shift, 1)
                together = jnp.where(lane_tile == index, moved, together)
                rows = pl.ds(pl.multiple_of(tile * SUB, SUB), SUB)
                word_stage[slot, block * SUB : (block + 1) * SUB, :] = words[passage, rows, :]
            code_stage[slot, row : row + 1, :] = together

    def decode(slot):
        for index in range(BLOCKS):
            word = word_stage[slot, index * SUB : (index + 1) * SUB, :]
            for field in range(FIELDS):
                rows = jnp.zeros((SUB, LANES), jnp.float32)
                for row in range(SUB):
                    place = index % row_blocks * tile_tokens + row * FIELDS + field
                    code = code_slots[slot][index // row_blocks, place]
                    rows = jnp.where(sub == row, table[pl.ds(code, SUB, stride=0), :], rows)
                low = jnp.bitwise_and(word, 1 << (2 * field)) != 0
                high = jnp.bitwise_and(word, 2 << (2 * field)) != 0
                residual = jnp.where(
                    high, jnp.where(low, level[3], level[2]), jnp.where(low, level[1], level[0])
                )
                base = index * tile_tokens + field * SUB
                dense[base : base + SUB, :] = rows + residual

    def normalize():
        for index in range(BLOCKS):
            rows = slice(index * tile_tokens, (index + 1) * tile_tokens)
            block = dense[rows, :]
            inverse = lax.rsqrt(jnp.sum(block * block, axis=1, keepdims=True) + 1e-06)
            embed[rows, :] = (block * inverse).astype(jnp.bfloat16)

    dense[...] = jnp.zeros(dense.shape, dense.dtype)
    embed[...] = jnp.zeros(embed.shape, embed.dtype)
    for slot in range(SLOTS):
        fetch(slot, slot)
        if slot < SLOTS - 1:
            slot_copy(slot).start()

    def step(group, carry):
        for slot in range(SLOTS):
            chunk = SLOTS * group + slot
            slot_copy(slot).wait()
            slot_copy((slot + SLOTS - 1) % SLOTS).start()

            @pl.when(chunk < chunks)
            def _(chunk=chunk, slot=slot):
                score(jnp.maximum(chunk - 2, 0))
                normalize()
                decode(slot)
                fetch(chunk + SLOTS, slot)

        return carry

    lax.fori_loop(0, (chunks + SLOTS - 1) // SLOTS, step, 0)
    for slot in range(SLOTS - 1):
        slot_copy(slot).wait()
    score(chunks - 2)
    normalize()
    score(chunks - 1)

    best = maxima[0, :items, :]
    for tile in range(1, tiles):
        best = jnp.maximum(best, maxima[tile, :items, :])
    sums = jnp.sum(best, axis=1, keepdims=True) / query_len
    item_down = lax.broadcasted_iota(jnp.int32, (items, LANES), 0)
    item_slot = lax.broadcasted_iota(jnp.int32, (items, LANES), 1)
    spread = jnp.where(item_down % capacity == item_slot, sums, 0.0)
    source_down = lax.broadcasted_iota(jnp.int32, (sources, items), 0)
    item_across = lax.broadcasted_iota(jnp.int32, (sources, items), 1)
    gather = (item_across // capacity == source_down).astype(jnp.float32)
    by_source = jnp.dot(
        gather, spread, precision=lax.Precision.HIGHEST, preferred_element_type=jnp.float32
    )
    best_lanes = token_best.shape[1]
    for source in range(sources):
        out_ref[source, :, :best_lanes] = token_best
        out_ref[source, :, best_lanes:] = by_source[source : source + 1, :]


def owner_scores(me, slots, query_parts, centroids, token_codes, resid_words, lengths, levels, sizes):
    capacity = sizes[4]
    sources = slots.shape[0]
    group_count = len(query_parts)
    group_rows = query_parts[0].shape[0]
    cent_dev, width = centroids.shape
    pass_dev, plen = token_codes.shape
    packed = resid_words.shape[1]
    tiles = packed // SUB
    items = sources * capacity
    quads = group_count * group_rows // LANES
    work_size = items * tiles + quads * ALIGN + (SLOTS + 1) * BLOCKS
    any_space = pl.BlockSpec(memory_space=pl.ANY)
    vmem = pl.BlockSpec(memory_space=pltpu.VMEM)
    tokens = items * plen
    return pl.pallas_call(
        functools.partial(score_kernel, sizes),
        in_specs=[pl.BlockSpec(memory_space=pltpu.SMEM)] * 2 + [vmem, vmem] + [any_space] * (4 + group_count),
        out_specs=vmem,
        out_shape=jax.ShapeDtypeStruct((sources, 1, group_rows + LANES), jnp.float32),
        scratch_shapes=[
            pltpu.VMEM((cent_dev, width), jnp.bfloat16),
            pltpu.VMEM((cent_dev + SUB, width), jnp.float32),
            pltpu.VMEM((pass_dev, packed, width), jnp.int32),
            pltpu.VMEM((group_count, group_rows, width), jnp.bfloat16),
            pltpu.VMEM((quads, width, LANES), jnp.bfloat16),
            pltpu.VMEM((width, group_rows), jnp.bfloat16),
            pltpu.VMEM((BLOCKS * SUB * FIELDS, width), jnp.float32),
            pltpu.VMEM((BLOCKS * SUB * FIELDS, width), jnp.bfloat16),
            pltpu.VMEM((tiles, items + SUB, LANES), jnp.float32),
            pltpu.VMEM((pass_dev, plen), jnp.int32),
            pltpu.VMEM((SLOTS, BLOCKS * SUB, LANES), jnp.int32),
            pltpu.VMEM((SLOTS, BLOCKS * SUB * FIELDS // LANES, LANES), jnp.int32),
            *[pltpu.SMEM((BLOCKS * SUB * FIELDS // LANES, LANES), jnp.int32)] * SLOTS,
            pltpu.SMEM((pass_dev,), jnp.int32),
            pltpu.SMEM((work_size,), jnp.int32),
            pltpu.SMEM((work_size // ALIGN + items * tiles // quads,), jnp.int32),
            pltpu.SMEM((items + 1,), jnp.int32),
            pltpu.SMEM((items + 1,), jnp.int32),
            pltpu.SMEM((items + 1,), jnp.int32),
            pltpu.SemaphoreType.DMA((quads,)),
            pltpu.SemaphoreType.DMA((4,)),
            pltpu.SemaphoreType.DMA((group_count,)),
            pltpu.SemaphoreType.DMA((2,)),
            pltpu.SemaphoreType.DMA((SLOTS,)),
        ],
        compiler_params=pltpu.CompilerParams(vmem_limit_bytes=56 * MIB),
        cost_estimate=pl.CostEstimate(
            flops=2 * (tokens * LANES + cent_dev * group_rows) * width, bytes_accessed=2 * cent_dev * width * 2, transcendentals=tokens
        ),
        name="owner_scores",
    )(
        me, slots, query_parts[0], levels, centroids, resid_words, token_codes, lengths, *query_parts
    )


def finish_kernel(sizes, me_ref, back_ref, target_ref, best_out, score_out):
    group_count, cent_count, _, query_len, capacity, _, _ = sizes
    group = jnp.bitwise_and(me_ref[0], group_count - 1)
    best_lanes = best_out.shape[0] * query_len
    best = back_ref[group, :, :best_lanes]
    for cent in range(1, cent_count):
        best = jnp.maximum(best, back_ref[cent * group_count + group, :, :best_lanes])
    for index in range(best_out.shape[0]):
        best_out[index : index + 1, :] = best[:, index * query_len : (index + 1) * query_len]
    back = back_ref[:, 0, best_lanes:]
    target = target_ref[...]
    owner = lax.broadcasted_iota(jnp.int32, (back.shape[0], target.shape[1]), 0)
    found = jnp.zeros(owner.shape, jnp.float32)
    for slot in range(capacity):
        found = found + jnp.where(owner * capacity + slot == target, back[:, slot : slot + 1], 0.0)
    scores = jnp.sum(found, axis=0, keepdims=True)
    width = score_out.shape[1]
    for index in range(score_out.shape[0]):
        score_out[index : index + 1, :] = scores[:, index * width : (index + 1) * width]


def finish(me, back, target, group_rows, sizes):
    _, _, per_device, query_len, _, _, cand_count = sizes
    vmem = pl.BlockSpec(memory_space=pltpu.VMEM)
    return pl.pallas_call(
        functools.partial(finish_kernel, sizes),
        in_specs=[pl.BlockSpec(memory_space=pltpu.SMEM), vmem, vmem],
        out_specs=[vmem] * 2,
        out_shape=[
            jax.ShapeDtypeStruct((group_rows, query_len), jnp.float32),
            jax.ShapeDtypeStruct((per_device, cand_count), jnp.float32),
        ],
        name="finish",
    )(me, back, target)


def shards(queries, centroids, candidates, token_codes, resid_words, lengths, levels):
    group_rows, query_len, width = queries.shape
    pass_dev = token_codes.shape[0]
    per_device, cand_count = candidates.shape[2:]
    pair_count = per_device * cand_count
    cent_count = lax.axis_size("cent")
    group_count = lax.axis_size("grp")
    devices = cent_count * group_count
    capacity = max(2, 2 * pair_count // devices)
    sizes = (group_count, cent_count, per_device, query_len, capacity, pass_dev, cand_count)
    cand = candidates.reshape(per_device, cand_count)
    query_rows = queries.reshape(group_rows * query_len, width)
    me = (lax.axis_index("cent") * group_count + lax.axis_index("grp")).astype(jnp.int32).reshape(1)
    slots, target = slots_by_owner(cand, devices, pass_dev, capacity)
    slots = lax.all_to_all(slots, ("cent", "grp"), split_axis=0, concat_axis=0, tiled=True)
    query_parts = [query_rows]
    for apart in range(1, group_count):
        pairs = [(index, index ^ apart) for index in range(group_count)]
        query_parts.append(lax.ppermute(query_rows, "grp", pairs))
    reply = owner_scores(
        me, slots, query_parts, centroids, token_codes, resid_words, lengths, levels, sizes
    )
    back = lax.all_to_all(reply, ("cent", "grp"), split_axis=0, concat_axis=0, tiled=True)
    token_best, scores = finish(me, back, target, group_rows, sizes)
    return (token_best, scores.reshape(1, 1, per_device, cand_count))


def solution(mesh):
    placed = (
        P("grp", None, None),
        P("cent", None),
        P("grp", "cent", None, None),
        P(("cent", "grp"), None),
        P(("cent", "grp"), None, None),
        P(("cent", "grp")),
        P(),
    )
    return jax.shard_map(
        shards,
        mesh=mesh,
        in_specs=placed,
        out_specs=(P("grp", None), P("grp", "cent", None, None)),
        check_vma=False,
    )
```

profile of v0, /device:TPU:0, one launch (start us, length us, event | category | flops | bytes accessed | tf_op | source)
XLA Modules:
  0.0 65.2 jit_solution(12591509876192755768)
XLA Ops:
  0.6 2.4 %collective-permute-start.2 = (bf16[512,128]{1,0:T(8,128)(2,1)}, bf16[512,128]{1,0:T(8,128)(2,1)S(1)}, u32[]{:S(2)}, u32[]{:S(2)}) collective-permute-start(bf16[512,128]{1,0:T(8,128)(2,1)} %bitcast.10), channel_id=1, source_target_pairs={{0,3},{1,2},{2,1},{3,0},{4,7},{5,6},{6,5},{7,4},{8,11},{9,10},{10,... | collective-permute-start | bytes 393224 | tf_op jit(solution)/shard_map/ppermute | solution.py:406
  3.1 0.6 collective-permute-start.1
  3.7 0.0 collective-permute-start
  3.8 1.6 %slots_by_owner.1 = (s32[32,8]{1,0:T(8,128)}, s32[1,128]{1,0:T(1,128)}) custom-call(s32[2,64]{1,0:T(2,128)} %bitcast.15), custom_call_target="tpu_custom_call" | custom-call | tf_op jit(solution)/shard_map/slots_by_owner/pallas_call | solution.py:56
  5.3 6.1 %all-to-all-start = ((s32[32,1,8]{2,1,0:T(1,128)}), s32[32,1,8]{2,1,0:T(1,128)S(1)}, u32[]{:S(2)}, u32[]{:S(2)}) async-start(s32[32,1,8]{2,1,0:T(1,128)} %bitcast.9), calls=%async_computation | async-start | bytes 32768 | tf_op jit(solution)/shard_map/all_to_all | solution.py:402
  11.4 7.1 %all-to-all-done = s32[32,1,8]{2,1,0:T(1,128)S(1)} async-done(((s32[32,1,8]{2,1,0:T(1,128)}), s32[32,1,8]{2,1,0:T(1,128)S(1)}, u32[]{:S(2)}, u32[]{:S(2)}) %all-to-all-start) | async-done | bytes 1056 | tf_op jit(solution)/shard_map/all_to_all | solution.py:402
  18.6 0.0 copy-start
  18.6 0.0 collective-permute-done.2.rest_3_
  18.6 0.0 copy-start.1
  18.6 0.0 collective-permute-done.1.rest_2_
  18.6 0.0 copy-start.2
  18.6 0.0 collective-permute-done.rest_1_
  18.6 0.0 copy-start.3
  18.6 0.6 copy-done
  19.2 0.1 copy-done.1
  19.3 0.1 copy-done.2
  19.3 0.0 copy-done.3
  19.4 20.7 %owner_scores.1 = f32[32,1,640]{2,1,0:T(1,128)} custom-call(s32[1]{0:T(128)} %bitcast.me_ref, s32[32,8]{1,0:T(8,128)} %bitcast.8, bf16[512,128]{1,0:T(8,128)(2,1)} %bitcast.13, f32[4,128]{1,0:T(4,128)} %levels_ref.1, bf16[32768,128]{1,0:T(8,128)(2,1)} %cent_hbm.1, s32[512,32,128]{2,1,0:T(8,128)} %words_hbm.1, s32[512,128]{1,0:T(8,128)} %codes_hbm.1, ...), custom_call_target="tpu_custom_call" | custom-call | flops 5368709120 | bytes 16777216 | tf_op jit(solution)/shard_map/owner_scores/pallas_call | solution.py:311
  40.1 23.2 %all_to_all.16.back_ref = f32[32,1,640]{2,1,0:T(1,128)} all-to-all(f32[32,1,640]{2,1,0:T(1,128)} %owner_scores.1), channel_id=1, replica_groups=mesh['cent'=8,'grp'=4] {'cent','grp'}, dimensions={0} | all-to-all | bytes 163840 | tf_op jit(solution)/shard_map/all_to_all | solution.py:410
  63.3 1.9 %finish.1 = (f32[16,32]{1,0:T(8,128)}, f32[2,64]{1,0:T(2,128)}) custom-call(s32[1]{0:T(128)} %bitcast.me_ref, f32[32,1,640]{2,1,0:T(1,128)} %all_to_all.16.back_ref, s32[1,128]{1,0:T(1,128)} %get-tuple-element.7.target_ref), custom_call_target="tpu_custom_call" | custom-call | tf_op jit(solution)/shard_map/finish/pallas_call | solution.py:376
Async XLA Ops:
  0.6 18.0 %collective-permute-start.2 = (bf16[512,128]{1,0:T(8,128)(2,1)}, bf16[512,128]{1,0:T(8,128)(2,1)S(1)}, u32[]{:S(2)}, u32[]{:S(2)}) collective-permute-start(bf16[512,128]{1,0:T(8,128)(2,1)} %bitcast.10), channel_id=1, source_target_pairs={{0,3},{1,2},{2,1},{3,0},{4,7},{5,6},{6,5},{7,4},{8,11},{9,10},{10,... | collective-permute-start | bytes 393224 | tf_op jit(solution)/shard_map/ppermute | solution.py:406
  3.1 15.5 %collective-permute-start.1 = (bf16[512,128]{1,0:T(8,128)(2,1)}, bf16[512,128]{1,0:T(8,128)(2,1)S(1)}, u32[]{:S(2)}, u32[]{:S(2)}) collective-permute-start(bf16[512,128]{1,0:T(8,128)(2,1)} %bitcast.11), channel_id=1, source_target_pairs={{0,2},{1,3},{2,0},{3,1},{4,6},{5,7},{6,4},{7,5},{8,10},{9,11},{10,... | collective-permute-start | bytes 393224 | tf_op jit(solution)/shard_map/ppermute | solution.py:406
  3.7 14.9 %collective-permute-start = (bf16[512,128]{1,0:T(8,128)(2,1)}, bf16[512,128]{1,0:T(8,128)(2,1)S(1)}, u32[]{:S(2)}, u32[]{:S(2)}) collective-permute-start(bf16[512,128]{1,0:T(8,128)(2,1)} %bitcast.12), channel_id=1, source_target_pairs={{0,1},{1,0},{2,3},{3,2},{4,5},{5,4},{6,7},{7,6},{8,9},{9,8},{10,11... | collective-permute-start | bytes 393224 | tf_op jit(solution)/shard_map/ppermute | solution.py:406
  5.3 13.3 %all-to-all-start = ((s32[32,1,8]{2,1,0:T(1,128)}), s32[32,1,8]{2,1,0:T(1,128)S(1)}, u32[]{:S(2)}, u32[]{:S(2)}) async-start(s32[32,1,8]{2,1,0:T(1,128)} %bitcast.9), calls=%async_computation | async-start | bytes 32768 | tf_op jit(solution)/shard_map/all_to_all | solution.py:402
  18.6 0.6 copy-start
  18.6 0.7 %copy-start.1 = (bf16[512,128]{1,0:T(8,128)(2,1)}, bf16[512,128]{1,0:T(8,128)(2,1)S(1)}, u32[]{:S(2)}) copy-start(bf16[512,128]{1,0:T(8,128)(2,1)S(1)} %collective-permute-done.2.rest_3_) | copy-start | bytes 393220
  18.6 0.7 %copy-start.2 = (bf16[512,128]{1,0:T(8,128)(2,1)}, bf16[512,128]{1,0:T(8,128)(2,1)S(1)}, u32[]{:S(2)}) copy-start(bf16[512,128]{1,0:T(8,128)(2,1)S(1)} %collective-permute-done.1.rest_2_) | copy-start | bytes 393220
  18.6 0.7 %copy-start.3 = (bf16[512,128]{1,0:T(8,128)(2,1)}, bf16[512,128]{1,0:T(8,128)(2,1)S(1)}, u32[]{:S(2)}) copy-start(bf16[512,128]{1,0:T(8,128)(2,1)S(1)} %collective-permute-done.rest_1_) | copy-start | bytes 393220
where the time goes:
time: 65.5 us; the launch traced here: 65.2 us
  Pallas kernels  24.2 us (37%)
  blocking collectives  23.2 us (35%)
  starting transfers between devices  9.22 us (14%)
  waiting for transfers between devices  7.15 us (11%)
  local copies, waits for them, and re-layouts  0.73 us (1%)
  between operations  0.69 us (1%)
    all_to_all x1, blocking collectives, shards(): lax.all_to_all(reply, ('cent', 'grp'), split_axis=0, concat_axis=0, tiled...  23.2 us
    pallas_call x1, Pallas kernels, owner_scores(): pl.pallas_call(functools.partial(score_kernel, sizes), in_specs=[pl.Block...  20.7 us
    all_to_all x1, waiting for transfers between devices, shards(): lax.all_to_all(slots, ('cent', 'grp'), split_axis=0, concat_axis=0, tiled...  7.14 us
    all_to_all x1, starting transfers between devices, shards(): lax.all_to_all(slots, ('cent', 'grp'), split_axis=0, concat_axis=0, tiled...  6.1 us
    ppermute x3, starting transfers between devices, shards(): query_parts.append(lax.ppermute(query_rows, 'grp', pairs))  3.12 us
    pallas_call x1, Pallas kernels, finish(): pl.pallas_call(functools.partial(finish_kernel, sizes), in_specs=[pl.Bloc...  1.91 us
    pallas_call x1, Pallas kernels, slots_by_owner(): pl.pallas_call(functools.partial(slots_kernel, pass_dev, capacity), in_sp...  1.58 us
  transfers between devices with their start and end apart: 4, of which 1 were waited for; matrix products, arithmetic and copies ran while one was open for 0% of the time, Pallas kernels for 2%

commit v1 on v0

--- a/solution.py
+++ b/solution.py
@@ -14,6 +14,7 @@
 BLOCKS = 16
 ALIGN = 8
 SLOTS = 4
+PARTS = 8
 MIB = 1 << 20
 
 
@@ -93,7 +94,9 @@
     group_quads = cent_count // quad_sources
     per_bits = per_device.bit_length() - 1
     tile_bits = tiles.bit_length() - 1
-    part_rows = staged.shape[0] // quads
+    parts = min(quads, PARTS)
+    part_rows = staged.shape[0] // parts
+    part_quads = quads // parts
     word_parts = words_sem.shape[0]
     part_pass = pass_dev // word_parts
 
@@ -121,7 +124,7 @@
     lens_copy.start()
     for apart in range(group_count):
         query_copy(apart).start()
-    lax.fori_loop(0, quads, start_table, 0)
+    lax.fori_loop(0, parts, start_table, 0)
     codes_copy.start()
     for part in range(word_parts):
         words_copy(part).start()
@@ -137,13 +140,7 @@
     item_lane[items] = -1
     spare = items * tiles
 
-    def prepare(quad, carry):
-        count, best = carry
-        table_copy(quad).wait()
-        rows = pl.ds(pl.multiple_of(quad * part_rows, part_rows), part_rows)
-        scores = jnp.dot(staged[rows, :], own_t[...], preferred_element_type=jnp.float32)
-        best = jnp.maximum(best, jnp.max(scores.reshape(part_rows // SUB, SUB, scores.shape[1]), axis=0))
-        table[rows, :] = staged[rows, :].astype(jnp.float32)
+    def fill(quad, count):
         block = query_rows[quad // group_quads, pl.ds(quad % group_quads * LANES, LANES), :]
         query_t[quad] = jnp.transpose(block.astype(jnp.float32)).astype(jnp.bfloat16)
         start = count
@@ -167,10 +164,21 @@
         count = (count + ALIGN - 1) // ALIGN * ALIGN
         for index in range(quad_sources * capacity * tiles // ALIGN):
             work_quad[start // ALIGN + index] = quad
+        return count
+
+    def prepare(part, carry):
+        count, best = carry
+        table_copy(part).wait()
+        rows = pl.ds(pl.multiple_of(part * part_rows, part_rows), part_rows)
+        scores = jnp.dot(staged[rows, :], own_t[...], preferred_element_type=jnp.float32)
+        best = jnp.maximum(best, jnp.max(scores.reshape(part_rows // SUB, SUB, scores.shape[1]), axis=0))
+        table[rows, :] = staged[rows, :].astype(jnp.float32)
+        for index in range(part_quads):
+            count = fill(part * part_quads + index, count)
         return count, best
 
     lowest = jnp.full((SUB, own_t.shape[1]), -jnp.inf, jnp.float32)
-    total, token_best = lax.fori_loop(0, quads, prepare, (0, lowest))
+    total, token_best = lax.fori_loop(0, parts, prepare, (0, lowest))
     token_best = jnp.max(token_best, axis=0, keepdims=True)
     for index in range((SLOTS + 1) * BLOCKS):
         work[total + index] = spare
@@ -249,17 +257,19 @@
     embed[...] = jnp.zeros(embed.shape, embed.dtype)
     for slot in range(SLOTS):
         fetch(slot, slot)
-        if slot < SLOTS - 1:
+        if slot < 2:
             slot_copy(slot).start()
+        elif slot < SLOTS - 1:
+            pl.when(slot < chunks)(slot_copy(slot).start)
 
     def step(group, carry):
         for slot in range(SLOTS):
             chunk = SLOTS * group + slot
-            slot_copy(slot).wait()
-            slot_copy((slot + SLOTS - 1) % SLOTS).start()
+            pl.when(chunk + SLOTS - 1 < chunks)(slot_copy((slot + SLOTS - 1) % SLOTS).start)
 
             @pl.when(chunk < chunks)
             def _(chunk=chunk, slot=slot):
+                slot_copy(slot).wait()
                 score(jnp.maximum(chunk - 2, 0))
                 normalize()
                 decode(slot)
@@ -268,8 +278,6 @@
         return carry
 
     lax.fori_loop(0, (chunks + SLOTS - 1) // SLOTS, step, 0)
-    for slot in range(SLOTS - 1):
-        slot_copy(slot).wait()
     score(chunks - 2)
     normalize()
     score(chunks - 1)
@@ -306,11 +314,16 @@
     quads = group_count * group_rows // LANES
     work_size = items * tiles + quads * ALIGN + (SLOTS + 1) * BLOCKS
     any_space = pl.BlockSpec(memory_space=pl.ANY)
+    in_hbm = pl.BlockSpec(memory_space=pltpu.HBM)
+    pinned = [
+        pltpu.with_memory_space_constraint(array, pltpu.HBM)
+        for array in (centroids, resid_words, token_codes, lengths)
+    ]
     vmem = pl.BlockSpec(memory_space=pltpu.VMEM)
     tokens = items * plen
     return pl.pallas_call(
         functools.partial(score_kernel, sizes),
-        in_specs=[pl.BlockSpec(memory_space=pltpu.SMEM)] * 2 + [vmem, vmem] + [any_space] * (4 + group_count),
+        in_specs=[pl.BlockSpec(memory_space=pltpu.SMEM)] * 2 + [vmem, vmem] + [in_hbm] * 4 + [any_space] * group_count,
         out_specs=vmem,
         out_shape=jax.ShapeDtypeStruct((sources, 1, group_rows + LANES), jnp.float32),
         scratch_shapes=[
@@ -333,19 +346,19 @@
             pltpu.SMEM((items + 1,), jnp.int32),
             pltpu.SMEM((items + 1,), jnp.int32),
             pltpu.SMEM((items + 1,), jnp.int32),
-            pltpu.SemaphoreType.DMA((quads,)),
+            pltpu.SemaphoreType.DMA((min(quads, PARTS),)),
             pltpu.SemaphoreType.DMA((4,)),
             pltpu.SemaphoreType.DMA((group_count,)),
             pltpu.SemaphoreType.DMA((2,)),
             pltpu.SemaphoreType.DMA((SLOTS,)),
         ],
-        compiler_params=pltpu.CompilerParams(vmem_limit_bytes=56 * MIB),
+        compiler_params=pltpu.CompilerParams(vmem_limit_bytes=44 * MIB),
         cost_estimate=pl.CostEstimate(
             flops=2 * (tokens * LANES + cent_dev * group_rows) * width, bytes_accessed=2 * cent_dev * width * 2, transcendentals=tokens
         ),
         name="owner_scores",
     )(
-        me, slots, query_parts[0], levels, centroids, resid_words, token_codes, lengths, *query_parts
+        me, slots, query_parts[0], levels, *pinned, *query_parts
     )
 
 

time: 65.5 us -> 66.4 us (1.014)
  Pallas kernels: 24.2 us -> 38 us
  blocking collectives: 23.2 us -> 10 us
  local copies, waits for them, and re-layouts: 0.73 us -> 1.58 us
    pallas_call x1, Pallas kernels: 20.7 us -> 34.5 us  [owner_scores(): pl.pallas_call(functools.partial(score_kernel, sizes), in_specs=[pl.Block...]
    all_to_all x1, blocking collectives: 23.2 us -> 10 us  [shards(): lax.all_to_all(reply, ('cent', 'grp'), split_axis=0, concat_axis=0, tiled...]
    unnamed x8 -> x4, local copies, waits for them, and re-layouts: 0.73 us -> 1.58 us
where the time goes in v1:
time: 66.4 us; the launch traced here: 66.6 us
  Pallas kernels  38 us (57%)
  blocking collectives  10 us (15%)
  starting transfers between devices  9.22 us (14%)
  waiting for transfers between devices  7.15 us (11%)
  local copies, waits for them, and re-layouts  1.58 us (2%)
  between operations  0.67 us (1%)
    pallas_call x1, Pallas kernels, owner_scores(): pl.pallas_call(functools.partial(score_kernel, sizes), in_specs=[pl.Block...  34.5 us
    all_to_all x1, blocking collectives, shards(): lax.all_to_all(reply, ('cent', 'grp'), split_axis=0, concat_axis=0, tiled...  10 us
    all_to_all x1, waiting for transfers between devices, shards(): lax.all_to_all(slots, ('cent', 'grp'), split_axis=0, concat_axis=0, tiled...  7.14 us
    all_to_all x1, starting transfers between devices, shards(): lax.all_to_all(slots, ('cent', 'grp'), split_axis=0, concat_axis=0, tiled...  6.1 us
    ppermute x3, starting transfers between devices, shards(): query_parts.append(lax.ppermute(query_rows, 'grp', pairs))  3.12 us
    pallas_call x1, Pallas kernels, finish(): pl.pallas_call(functools.partial(finish_kernel, sizes), in_specs=[pl.Bloc...  1.91 us
    unnamed x4, local copies, waits for them, and re-layouts  1.58 us
    pallas_call x1, Pallas kernels, slots_by_owner(): pl.pallas_call(functools.partial(slots_kernel, pass_dev, capacity), in_sp...  1.57 us
  transfers between devices with their start and end apart: 4, of which 1 were waited for; matrix products, arithmetic and copies ran while one was open for 0% of the time, Pallas kernels for 2%

profile of v1, /device:TPU:0, one launch (start us, length us, event | category | flops | bytes accessed | tf_op | source)
XLA Modules:
  0.0 66.6 jit_solution(10398056205479714607)
XLA Ops:
  0.6 2.4 %collective-permute-start.2 = (bf16[512,128]{1,0:T(8,128)(2,1)}, bf16[512,128]{1,0:T(8,128)(2,1)S(1)}, u32[]{:S(2)}, u32[]{:S(2)}) collective-permute-start(bf16[512,128]{1,0:T(8,128)(2,1)} %bitcast.9), channel_id=1, source_target_pairs={{0,3},{1,2},{2,1},{3,0},{4,7},{5,6},{6,5},{7,4},{8,11},{9,10},{10,... | collective-permute-start | bytes 393224 | tf_op jit(solution)/shard_map/ppermute | solution.py:419
  3.1 0.6 collective-permute-start.1
  3.7 0.0 collective-permute-start
  3.8 1.6 %slots_by_owner.1 = (s32[32,8]{1,0:T(8,128)}, s32[1,128]{1,0:T(1,128)}) custom-call(s32[2,64]{1,0:T(2,128)} %bitcast.15), custom_call_target="tpu_custom_call" | custom-call | tf_op jit(solution)/shard_map/slots_by_owner/pallas_call | solution.py:57
  5.3 6.1 %all-to-all-start = ((s32[32,1,8]{2,1,0:T(1,128)}), s32[32,1,8]{2,1,0:T(1,128)S(1)}, u32[]{:S(2)}, u32[]{:S(2)}) async-start(s32[32,1,8]{2,1,0:T(1,128)} %bitcast.14), calls=%async_computation | async-start | bytes 32768 | tf_op jit(solution)/shard_map/all_to_all | solution.py:415
  11.4 7.1 %all-to-all-done = s32[32,1,8]{2,1,0:T(1,128)S(1)} async-done(((s32[32,1,8]{2,1,0:T(1,128)}), s32[32,1,8]{2,1,0:T(1,128)S(1)}, u32[]{:S(2)}, u32[]{:S(2)}) %all-to-all-start) | async-done | bytes 1056 | tf_op jit(solution)/shard_map/all_to_all | solution.py:415
  18.6 0.0 collective-permute-done.2.rest_3_
  18.6 0.0 collective-permute-done.1.rest_2_
  18.6 0.0 collective-permute-done.rest_1_
  18.6 0.0 copy-start
  18.6 0.9 %copy-done = bf16[16,32,128]{2,1,0:T(8,128)(2,1)S(1)} copy-done((bf16[16,32,128]{2,1,0:T(8,128)(2,1)S(1)}, bf16[16,32,128]{2,1,0:T(8,128)(2,1)}, u32[]{:S(2)}) %copy-start) | copy-done | bytes 131096
  19.5 0.0 copy-start.1
  19.5 0.7 %copy-done.1 = f32[4,128]{1,0:T(4,128)S(1)} copy-done((f32[4,128]{1,0:T(4,128)S(1)}, f32[4,128]{1,0:T(4,128)}, u32[]{:S(2)}) %copy-start.1) | copy-done | bytes 2072
  20.2 34.5 %owner_scores.1 = f32[32,1,640]{2,1,0:T(1,128)S(1)} custom-call(s32[1]{0:T(128)} %bitcast.me_ref, s32[32,8]{1,0:T(8,128)S(1)} %bitcast.8, bf16[512,128]{1,0:T(8,128)(2,1)S(1)} %bitcast.12, f32[4,128]{1,0:T(4,128)S(1)} %copy-done.1, bf16[32768,128]{1,0:T(8,128)(2,1)} %cent_hbm.1, s32[512,32,128]{2,1,0:T(8,128)} %words_hbm.1, s32[512,128]{1,0:T(8,128)} %codes_hbm.1, ...), custom_call_target="tpu_custom_call" | custom-call | flops 5368709120 | bytes 16777216 | tf_op jit(solution)/shard_map/owner_scores/pallas_call | solution.py:324
  54.7 10.0 %all_to_all.16.back_ref = f32[32,1,640]{2,1,0:T(1,128)} all-to-all(f32[32,1,640]{2,1,0:T(1,128)S(1)} %owner_scores.1), channel_id=1, replica_groups=mesh['cent'=8,'grp'=4] {'cent','grp'}, dimensions={0} | all-to-all | bytes 163840 | tf_op jit(solution)/shard_map/all_to_all | solution.py:423
  64.7 1.9 %finish.1 = (f32[16,32]{1,0:T(8,128)}, f32[2,64]{1,0:T(2,128)}) custom-call(s32[1]{0:T(128)} %bitcast.me_ref, f32[32,1,640]{2,1,0:T(1,128)} %all_to_all.16.back_ref, s32[1,128]{1,0:T(1,128)} %get-tuple-element.7.target_ref), custom_call_target="tpu_custom_call" | custom-call | tf_op jit(solution)/shard_map/finish/pallas_call | solution.py:389
Async XLA Ops:
  0.6 17.9 %collective-permute-start.2 = (bf16[512,128]{1,0:T(8,128)(2,1)}, bf16[512,128]{1,0:T(8,128)(2,1)S(1)}, u32[]{:S(2)}, u32[]{:S(2)}) collective-permute-start(bf16[512,128]{1,0:T(8,128)(2,1)} %bitcast.9), channel_id=1, source_target_pairs={{0,3},{1,2},{2,1},{3,0},{4,7},{5,6},{6,5},{7,4},{8,11},{9,10},{10,... | collective-permute-start | bytes 393224 | tf_op jit(solution)/shard_map/ppermute | solution.py:419
  3.1 15.5 %collective-permute-start.1 = (bf16[512,128]{1,0:T(8,128)(2,1)}, bf16[512,128]{1,0:T(8,128)(2,1)S(1)}, u32[]{:S(2)}, u32[]{:S(2)}) collective-permute-start(bf16[512,128]{1,0:T(8,128)(2,1)} %bitcast.10), channel_id=1, source_target_pairs={{0,2},{1,3},{2,0},{3,1},{4,6},{5,7},{6,4},{7,5},{8,10},{9,11},{10,... | collective-permute-start | bytes 393224 | tf_op jit(solution)/shard_map/ppermute | solution.py:419
  3.7 14.9 %collective-permute-start = (bf16[512,128]{1,0:T(8,128)(2,1)}, bf16[512,128]{1,0:T(8,128)(2,1)S(1)}, u32[]{:S(2)}, u32[]{:S(2)}) collective-permute-start(bf16[512,128]{1,0:T(8,128)(2,1)} %bitcast.11), channel_id=1, source_target_pairs={{0,1},{1,0},{2,3},{3,2},{4,5},{5,4},{6,7},{7,6},{8,9},{9,8},{10,11... | collective-permute-start | bytes 393224 | tf_op jit(solution)/shard_map/ppermute | solution.py:419
  5.3 13.3 %all-to-all-start = ((s32[32,1,8]{2,1,0:T(1,128)}), s32[32,1,8]{2,1,0:T(1,128)S(1)}, u32[]{:S(2)}, u32[]{:S(2)}) async-start(s32[32,1,8]{2,1,0:T(1,128)} %bitcast.14), calls=%async_computation | async-start | bytes 32768 | tf_op jit(solution)/shard_map/all_to_all | solution.py:415
  18.6 0.9 %copy-start = (bf16[16,32,128]{2,1,0:T(8,128)(2,1)S(1)}, bf16[16,32,128]{2,1,0:T(8,128)(2,1)}, u32[]{:S(2)}) copy-start(bf16[16,32,128]{2,1,0:T(8,128)(2,1)} %param.7) | copy-start | bytes 393220
  19.5 0.7 %copy-start.1 = (f32[4,128]{1,0:T(4,128)S(1)}, f32[4,128]{1,0:T(4,128)}, u32[]{:S(2)}) copy-start(f32[4,128]{1,0:T(4,128)} %levels_ref.1) | copy-start | bytes 6148

commit v2 on v1

--- a/solution.py
+++ b/solution.py
@@ -12,7 +12,7 @@
 SUB = 8
 FIELDS = 4
 BLOCKS = 16
-ALIGN = 8
+ALIGN = 4
 SLOTS = 4
 PARTS = 8
 MIB = 1 << 20
@@ -70,8 +70,7 @@
     sizes,
     me_ref,
     ids,
-    own_ref,
-    levels_ref,
+    levels_hbm,
     cent_hbm,
     words_hbm,
     codes_hbm,
@@ -83,7 +82,7 @@
     (out_ref, staged, table, words, query_rows, query_t, own_t, dense, embed, maxima, codes, word_stage,
      code_stage, *more) = rest[group_count:]
     code_slots, more = more[:SLOTS], more[SLOTS:]
-    (lens, work, work_quad, item_pass, item_len, item_lane, table_sem, words_sem, query_sem, small_sem,
+    (levels_ref, lens, work, work_quad, item_pass, item_len, item_lane, table_sem, words_sem, query_sem, small_sem,
      slot_sem) = more
     sources = ids.shape[0]
     items = sources * capacity
@@ -121,7 +120,9 @@
 
     lens_copy = pltpu.make_async_copy(lens_hbm, lens, small_sem.at[0])
     codes_copy = pltpu.make_async_copy(codes_hbm, codes, small_sem.at[1])
+    levels_copy = pltpu.make_async_copy(levels_hbm, levels_ref, small_sem.at[2])
     lens_copy.start()
+    levels_copy.start()
     for apart in range(group_count):
         query_copy(apart).start()
     lax.fori_loop(0, parts, start_table, 0)
@@ -130,9 +131,10 @@
         words_copy(part).start()
 
     maxima[...] = jnp.full(maxima.shape, MASKED, jnp.float32)
-    own_t[...] = jnp.transpose(own_ref[...].astype(jnp.float32)).astype(jnp.bfloat16)
+    query_copy(0).wait()
+    own_t[...] = jnp.transpose(query_rows[group].astype(jnp.float32)).astype(jnp.bfloat16)
     lens_copy.wait()
-    for apart in range(group_count):
+    for apart in range(1, group_count):
         query_copy(apart).wait()
 
     item_pass[items] = 0
@@ -186,6 +188,7 @@
         work_quad[total // ALIGN + index] = 0
     chunks = jnp.maximum((total + BLOCKS - 1) // BLOCKS, 2)
     codes_copy.wait()
+    levels_copy.wait()
     for part in range(word_parts):
         words_copy(part).wait()
 
@@ -214,20 +217,25 @@
     def slot_copy(slot):
         return pltpu.make_async_copy(code_stage.at[slot], code_slots[slot], slot_sem.at[slot])
 
-    def fetch(chunk, slot):
+    def fetch_codes(chunk, slot):
+        places = []
         for row in range(BLOCKS // row_blocks):
             together = jnp.zeros((1, LANES), jnp.int32)
             for index in range(row_blocks):
-                block = row * row_blocks + index
-                entry = work[chunk * BLOCKS + block]
+                entry = work[chunk * BLOCKS + row * row_blocks + index]
                 passage = item_pass[jnp.right_shift(entry, tile_bits)]
                 tile = jnp.bitwise_and(entry, tiles - 1)
                 shift = jnp.bitwise_and(index - tile, row_blocks - 1) * tile_tokens
                 moved = pltpu.roll(codes[pl.ds(passage, 1), :], shift, 1)
                 together = jnp.where(lane_tile == index, moved, together)
-                rows = pl.ds(pl.multiple_of(tile * SUB, SUB), SUB)
-                word_stage[slot, block * SUB : (block + 1) * SUB, :] = words[passage, rows, :]
+                places.append((passage, tile))
             code_stage[slot, row : row + 1, :] = together
+        return places
+
+    def fetch_words(places, slot):
+        for block, (passage, tile) in enumerate(places):
+            rows = pl.ds(pl.multiple_of(tile * SUB, SUB), SUB)
+            word_stage[slot, block * SUB : (block + 1) * SUB, :] = words[passage, rows, :]
 
     def decode(slot):
         for index in range(BLOCKS):
@@ -256,7 +264,7 @@
     dense[...] = jnp.zeros(dense.shape, dense.dtype)
     embed[...] = jnp.zeros(embed.shape, embed.dtype)
     for slot in range(SLOTS):
-        fetch(slot, slot)
+        fetch_words(fetch_codes(slot, slot), slot)
         if slot < 2:
             slot_copy(slot).start()
         elif slot < SLOTS - 1:
@@ -272,8 +280,9 @@
                 slot_copy(slot).wait()
                 score(jnp.maximum(chunk - 2, 0))
                 normalize()
+                places = fetch_codes(chunk + SLOTS, slot)
                 decode(slot)
-                fetch(chunk + SLOTS, slot)
+                fetch_words(places, slot)
 
         return carry
 
@@ -317,13 +326,13 @@
     in_hbm = pl.BlockSpec(memory_space=pltpu.HBM)
     pinned = [
         pltpu.with_memory_space_constraint(array, pltpu.HBM)
-        for array in (centroids, resid_words, token_codes, lengths)
+        for array in (levels, centroids, resid_words, token_codes, lengths, query_parts[0])
     ]
     vmem = pl.BlockSpec(memory_space=pltpu.VMEM)
     tokens = items * plen
     return pl.pallas_call(
         functools.partial(score_kernel, sizes),
-        in_specs=[pl.BlockSpec(memory_space=pltpu.SMEM)] * 2 + [vmem, vmem] + [in_hbm] * 4 + [any_space] * group_count,
+        in_specs=[pl.BlockSpec(memory_space=pltpu.SMEM)] * 2 + [in_hbm] * 6 + [any_space] * (group_count - 1),
         out_specs=vmem,
         out_shape=jax.ShapeDtypeStruct((sources, 1, group_rows + LANES), jnp.float32),
         scratch_shapes=[
@@ -340,6 +349,7 @@
             pltpu.VMEM((SLOTS, BLOCKS * SUB, LANES), jnp.int32),
             pltpu.VMEM((SLOTS, BLOCKS * SUB * FIELDS // LANES, LANES), jnp.int32),
             *[pltpu.SMEM((BLOCKS * SUB * FIELDS // LANES, LANES), jnp.int32)] * SLOTS,
+            pltpu.VMEM(levels.shape, jnp.float32),
             pltpu.SMEM((pass_dev,), jnp.int32),
             pltpu.SMEM((work_size,), jnp.int32),
             pltpu.SMEM((work_size // ALIGN + items * tiles // quads,), jnp.int32),
@@ -349,7 +359,7 @@
             pltpu.SemaphoreType.DMA((min(quads, PARTS),)),
             pltpu.SemaphoreType.DMA((4,)),
             pltpu.SemaphoreType.DMA((group_count,)),
-            pltpu.SemaphoreType.DMA((2,)),
+            pltpu.SemaphoreType.DMA((3,)),
             pltpu.SemaphoreType.DMA((SLOTS,)),
         ],
         compiler_params=pltpu.CompilerParams(vmem_limit_bytes=44 * MIB),
@@ -358,7 +368,7 @@
         ),
         name="owner_scores",
     )(
-        me, slots, query_parts[0], levels, *pinned, *query_parts
+        me, slots, *pinned, *query_parts[1:]
     )
 
 

time: 66.4 us -> 63 us (0.949); the launches traced: 66.6 us -> 62.1 us
  Pallas kernels: 38 us -> 29.6 us
  blocking collectives: 10 us -> 15.5 us
  local copies, waits for them, and re-layouts: 1.58 us -> 0 us
    pallas_call x1, Pallas kernels: 34.5 us -> 26.2 us  [owner_scores(): pl.pallas_call(functools.partial(score_kernel, sizes), in_specs=[pl.Block...]
    all_to_all x1, blocking collectives: 10 us -> 15.5 us  [shards(): lax.all_to_all(reply, ('cent', 'grp'), split_axis=0, concat_axis=0, tiled...]
    unnamed x4 -> x0, local copies, waits for them, and re-layouts: 1.58 us -> none
  transfers between devices with their start and end apart: 4 -> 4, of which waited for: 1 -> 1; matrix products, arithmetic and copies ran while one was open for 0% -> 0% of each run, Pallas kernels for 2% -> 3%
where the time goes in v2:
time: 63 us; the launch traced here: 62.1 us
  Pallas kernels  29.6 us (47%)
  blocking collectives  15.5 us (25%)
  starting transfers between devices  9.22 us (15%)
  waiting for transfers between devices  7.15 us (11%)
  between operations  0.66 us (1%)
    pallas_call x1, Pallas kernels, owner_scores(): pl.pallas_call(functools.partial(score_kernel, sizes), in_specs=[pl.Block...  26.2 us
    all_to_all x1, blocking collectives, shards(): lax.all_to_all(reply, ('cent', 'grp'), split_axis=0, concat_axis=0, tiled...  15.5 us
    all_to_all x1, waiting for transfers between devices, shards(): lax.all_to_all(slots, ('cent', 'grp'), split_axis=0, concat_axis=0, tiled...  7.14 us
    all_to_all x1, starting transfers between devices, shards(): lax.all_to_all(slots, ('cent', 'grp'), split_axis=0, concat_axis=0, tiled...  6.1 us
    ppermute x3, starting transfers between devices, shards(): query_parts.append(lax.ppermute(query_rows, 'grp', pairs))  3.12 us
    pallas_call x1, Pallas kernels, finish(): pl.pallas_call(functools.partial(finish_kernel, sizes), in_specs=[pl.Bloc...  1.91 us
    pallas_call x1, Pallas kernels, slots_by_owner(): pl.pallas_call(functools.partial(slots_kernel, pass_dev, capacity), in_sp...  1.57 us
  transfers between devices with their start and end apart: 4, of which 1 were waited for; matrix products, arithmetic and copies ran while one was open for 0% of the time, Pallas kernels for 3%

profile of v2, /device:TPU:0, one launch (start us, length us, event | category | flops | bytes accessed | tf_op | source)
XLA Modules:
  0.0 62.1 jit_solution(15197678104991364719)
XLA Ops:
  0.6 2.4 %collective-permute-start.2 = (bf16[512,128]{1,0:T(8,128)(2,1)}, bf16[512,128]{1,0:T(8,128)(2,1)S(1)}, u32[]{:S(2)}, u32[]{:S(2)}) collective-permute-start(bf16[512,128]{1,0:T(8,128)(2,1)} %bitcast.10), channel_id=1, source_target_pairs={{0,3},{1,2},{2,1},{3,0},{4,7},{5,6},{6,5},{7,4},{8,11},{9,10},{10,... | collective-permute-start | bytes 393224 | tf_op jit(solution)/shard_map/ppermute | solution.py:429
  3.1 0.6 %collective-permute-start.1 = (bf16[512,128]{1,0:T(8,128)(2,1)}, bf16[512,128]{1,0:T(8,128)(2,1)S(1)}, u32[]{:S(2)}, u32[]{:S(2)}) collective-permute-start(bf16[512,128]{1,0:T(8,128)(2,1)} %bitcast.11), channel_id=1, source_target_pairs={{0,2},{1,3},{2,0},{3,1},{4,6},{5,7},{6,4},{7,5},{8,10},{9,11},{10,... | collective-permute-start | bytes 393224 | tf_op jit(solution)/shard_map/ppermute | solution.py:429
  3.7 0.0 collective-permute-start
  3.8 1.6 %slots_by_owner.1 = (s32[32,8]{1,0:T(8,128)}, s32[1,128]{1,0:T(1,128)}) custom-call(s32[2,64]{1,0:T(2,128)} %bitcast.14), custom_call_target="tpu_custom_call" | custom-call | tf_op jit(solution)/shard_map/slots_by_owner/pallas_call | solution.py:57
  5.3 6.1 %all-to-all-start = ((s32[32,1,8]{2,1,0:T(1,128)}), s32[32,1,8]{2,1,0:T(1,128)S(1)}, u32[]{:S(2)}, u32[]{:S(2)}) async-start(s32[32,1,8]{2,1,0:T(1,128)} %bitcast.9), calls=%async_computation | async-start | bytes 32768 | tf_op jit(solution)/shard_map/all_to_all | solution.py:425
  11.4 7.1 %all-to-all-done = s32[32,1,8]{2,1,0:T(1,128)S(1)} async-done(((s32[32,1,8]{2,1,0:T(1,128)}), s32[32,1,8]{2,1,0:T(1,128)S(1)}, u32[]{:S(2)}, u32[]{:S(2)}) %all-to-all-start) | async-done | bytes 1056 | tf_op jit(solution)/shard_map/all_to_all | solution.py:425
  18.6 0.0 collective-permute-done.2.rest_3_
  18.6 0.0 collective-permute-done.1.rest_2_
  18.6 0.0 collective-permute-done.rest_1_
  18.6 26.2 %owner_scores.1 = f32[32,1,640]{2,1,0:T(1,128)S(1)} custom-call(s32[1]{0:T(128)} %bitcast.me_ref, s32[32,8]{1,0:T(8,128)S(1)} %bitcast.8, f32[4,128]{1,0:T(4,128)} %levels_hbm.1, bf16[32768,128]{1,0:T(8,128)(2,1)} %cent_hbm.1, s32[512,32,128]{2,1,0:T(8,128)} %words_hbm.1, s32[512,128]{1,0:T(8,128)} %codes_hbm.1, s32[512]{0:T(512)} %lens_hbm.1, ...), custom_call_target="tpu_custom_call" | custom-call | flops 5368709120 | bytes 16777216 | tf_op jit(solution)/shard_map/owner_scores/pallas_call | solution.py:333
  44.8 15.5 %all_to_all.16.back_ref = f32[32,1,640]{2,1,0:T(1,128)} all-to-all(f32[32,1,640]{2,1,0:T(1,128)S(1)} %owner_scores.1), channel_id=1, replica_groups=mesh['cent'=8,'grp'=4] {'cent','grp'}, dimensions={0} | all-to-all | bytes 163840 | tf_op jit(solution)/shard_map/all_to_all | solution.py:433
  60.2 1.9 %finish.1 = (f32[16,32]{1,0:T(8,128)}, f32[2,64]{1,0:T(2,128)}) custom-call(s32[1]{0:T(128)} %bitcast.me_ref, f32[32,1,640]{2,1,0:T(1,128)} %all_to_all.16.back_ref, s32[1,128]{1,0:T(1,128)} %get-tuple-element.7.target_ref), custom_call_target="tpu_custom_call" | custom-call | tf_op jit(solution)/shard_map/finish/pallas_call | solution.py:399
Async XLA Ops:
  0.6 18.0 %collective-permute-start.2 = (bf16[512,128]{1,0:T(8,128)(2,1)}, bf16[512,128]{1,0:T(8,128)(2,1)S(1)}, u32[]{:S(2)}, u32[]{:S(2)}) collective-permute-start(bf16[512,128]{1,0:T(8,128)(2,1)} %bitcast.10), channel_id=1, source_target_pairs={{0,3},{1,2},{2,1},{3,0},{4,7},{5,6},{6,5},{7,4},{8,11},{9,10},{10,... | collective-permute-start | bytes 393224 | tf_op jit(solution)/shard_map/ppermute | solution.py:429
  3.1 15.5 %collective-permute-start.1 = (bf16[512,128]{1,0:T(8,128)(2,1)}, bf16[512,128]{1,0:T(8,128)(2,1)S(1)}, u32[]{:S(2)}, u32[]{:S(2)}) collective-permute-start(bf16[512,128]{1,0:T(8,128)(2,1)} %bitcast.11), channel_id=1, source_target_pairs={{0,2},{1,3},{2,0},{3,1},{4,6},{5,7},{6,4},{7,5},{8,10},{9,11},{10,... | collective-permute-start | bytes 393224 | tf_op jit(solution)/shard_map/ppermute | solution.py:429
  3.7 14.9 %collective-permute-start = (bf16[512,128]{1,0:T(8,128)(2,1)}, bf16[512,128]{1,0:T(8,128)(2,1)S(1)}, u32[]{:S(2)}, u32[]{:S(2)}) collective-permute-start(bf16[512,128]{1,0:T(8,128)(2,1)} %bitcast.12), channel_id=1, source_target_pairs={{0,1},{1,0},{2,3},{3,2},{4,5},{5,4},{6,7},{7,6},{8,9},{9,8},{10,11... | collective-permute-start | bytes 393224 | tf_op jit(solution)/shard_map/ppermute | solution.py:429
  5.3 13.3 %all-to-all-start = ((s32[32,1,8]{2,1,0:T(1,128)}), s32[32,1,8]{2,1,0:T(1,128)S(1)}, u32[]{:S(2)}, u32[]{:S(2)}) async-start(s32[32,1,8]{2,1,0:T(1,128)} %bitcast.9), calls=%async_computation | async-start | bytes 32768 | tf_op jit(solution)/shard_map/all_to_all | solution.py:425

commit v3 on v2

--- a/solution.py
+++ b/solution.py
@@ -82,30 +82,35 @@
     (out_ref, staged, table, words, query_rows, query_t, own_t, dense, embed, maxima, codes, word_stage,
      code_stage, *more) = rest[group_count:]
     code_slots, more = more[:SLOTS], more[SLOTS:]
-    (levels_ref, lens, work, work_quad, item_pass, item_len, item_lane, table_sem, words_sem, query_sem, small_sem,
+    (levels_ref, lens, work, work_quad, table_sem, words_sem, query_sem, small_sem,
      slot_sem) = more
     sources = ids.shape[0]
     items = sources * capacity
-    tiles = words.shape[1] // SUB
+    tiles = words.shape[0] // (pass_dev * SUB)
     tile_tokens = SUB * FIELDS
     quad_sources = LANES // (per_device * query_len)
     quads = sources // quad_sources
     group_quads = cent_count // quad_sources
     per_bits = per_device.bit_length() - 1
     tile_bits = tiles.bit_length() - 1
+    row_at = (pass_dev * tiles - 1).bit_length()
+    lane_at = row_at + (items * tiles).bit_length()
+    last_at = lane_at + (quad_sources * per_device - 1).bit_length()
+    assert last_at + (tiles * tile_tokens - 1).bit_length() < 32
+    next_tile = 1 + (1 << row_at) - (tile_tokens << last_at)
     parts = min(quads, PARTS)
     part_rows = staged.shape[0] // parts
     part_quads = quads // parts
     word_parts = words_sem.shape[0]
-    part_pass = pass_dev // word_parts
+    part_words = words.shape[0] // word_parts
 
     def table_copy(part):
         rows = pl.ds(pl.multiple_of(part * part_rows, part_rows), part_rows)
         return pltpu.make_async_copy(cent_hbm.at[rows, :], staged.at[rows, :], table_sem.at[part])
 
     def words_copy(part):
-        rows = pl.ds(part * part_pass, part_pass)
-        return pltpu.make_async_copy(words_hbm.at[rows], words.at[rows], words_sem.at[part])
+        rows = pl.ds(part * part_words, part_words)
+        return pltpu.make_async_copy(words_hbm.at[rows, :], words.at[rows, :], words_sem.at[part])
 
     def start_table(part, carry):
         table_copy(part).start()
@@ -137,10 +142,7 @@
     for apart in range(1, group_count):
         query_copy(apart).wait()
 
-    item_pass[items] = 0
-    item_len[items] = 0
-    item_lane[items] = -1
-    spare = items * tiles
+    spare = ((items * tiles) << row_at) - (1 << last_at)
 
     def fill(quad, count):
         block = query_rows[quad // group_quads, pl.ds(quad % group_quads * LANES, LANES), :]
@@ -150,15 +152,17 @@
         for part in range(quad_sources):
             cent = quad % group_quads * quad_sources + part
             source = cent * group_count + quad // group_quads
-            found += [(part, source * capacity + slot, ids[source, slot] - 1) for slot in range(capacity)]
-        found = [(part, item, tag, jnp.maximum(tag, 0)) for part, item, tag in found]
-        lengths = [lens[jnp.right_shift(held, per_bits)] for _, _, _, held in found]
-        for (part, item, tag, held), length in zip(found, lengths):
-            item_pass[item] = jnp.right_shift(held, per_bits)
-            item_len[item] = length
-            item_lane[item] = part * per_device + jnp.bitwise_and(held, per_device - 1)
+            rows = jnp.left_shift(source * (capacity * tiles), row_at)
+            for slot in range(capacity):
+                tag = ids[source, slot] - 1
+                lane = part * per_device + jnp.bitwise_and(tag, per_device - 1)
+                entry = rows + jnp.left_shift(lane, lane_at) + ((slot * tiles) << row_at)
+                found.append((tag, jnp.right_shift(jnp.maximum(tag, 0), per_bits), entry))
+        lengths = [lens[passage] for _, passage, _ in found]
+        for (tag, passage, entry), length in zip(found, lengths):
+            entry = entry + jnp.left_shift(passage, tile_bits) + jnp.left_shift(length - 1, last_at)
             for tile in range(tiles):
-                work[count + tile] = item * tiles + tile
+                work[count + tile] = entry + tile * next_tile
             blocks = jnp.right_shift(length + tile_tokens - 1, tile_tokens.bit_length() - 1)
             count = count + jnp.where(tag >= 0, blocks, 0)
         for index in range(ALIGN):
@@ -207,12 +211,13 @@
             scores.append(jnp.dot(rows, query_t[quad], preferred_element_type=jnp.float32))
         for index in range(BLOCKS):
             entry = work[chunk * BLOCKS + index]
-            item, tile = jnp.right_shift(entry, tile_bits), jnp.bitwise_and(entry, tiles - 1)
             inner = index % ALIGN
             block = scores[index // ALIGN][inner * tile_tokens : (inner + 1) * tile_tokens]
-            kept = jnp.where(position < item_len[item] - tile * tile_tokens, block, MASKED)
+            kept = jnp.where(position <= jnp.right_shift(entry, last_at), block, MASKED)
             best = jnp.max(kept, axis=0, keepdims=True)
-            maxima[tile, pl.ds(item, 1), :] = jnp.where(lane_group == item_lane[item], best, 0.0)
+            row = jnp.bitwise_and(jnp.right_shift(entry, row_at), (1 << (lane_at - row_at)) - 1)
+            lane = jnp.bitwise_and(jnp.right_shift(entry, lane_at), (1 << (last_at - lane_at)) - 1)
+            maxima[pl.ds(row, 1), :] = jnp.where(lane_group == lane, best, 0.0)
 
     def slot_copy(slot):
         return pltpu.make_async_copy(code_stage.at[slot], code_slots[slot], slot_sem.at[slot])
@@ -223,19 +228,19 @@
             together = jnp.zeros((1, LANES), jnp.int32)
             for index in range(row_blocks):
                 entry = work[chunk * BLOCKS + row * row_blocks + index]
-                passage = item_pass[jnp.right_shift(entry, tile_bits)]
-                tile = jnp.bitwise_and(entry, tiles - 1)
-                shift = jnp.bitwise_and(index - tile, row_blocks - 1) * tile_tokens
+                place = jnp.bitwise_and(entry, (1 << row_at) - 1)
+                passage = jnp.right_shift(place, tile_bits)
+                shift = jnp.bitwise_and(index - place, row_blocks - 1) * tile_tokens
                 moved = pltpu.roll(codes[pl.ds(passage, 1), :], shift, 1)
                 together = jnp.where(lane_tile == index, moved, together)
-                places.append((passage, tile))
+                places.append(place)
             code_stage[slot, row : row + 1, :] = together
         return places
 
     def fetch_words(places, slot):
-        for block, (passage, tile) in enumerate(places):
-            rows = pl.ds(pl.multiple_of(tile * SUB, SUB), SUB)
-            word_stage[slot, block * SUB : (block + 1) * SUB, :] = words[passage, rows, :]
+        for block, place in enumerate(places):
+            rows = pl.ds(pl.multiple_of(place * SUB, SUB), SUB)
+            word_stage[slot, block * SUB : (block + 1) * SUB, :] = words[rows, :]
 
     def decode(slot):
         for index in range(BLOCKS):
@@ -291,9 +296,9 @@
     normalize()
     score(chunks - 1)
 
-    best = maxima[0, :items, :]
+    best = maxima[pl.ds(0, items, stride=tiles), :]
     for tile in range(1, tiles):
-        best = jnp.maximum(best, maxima[tile, :items, :])
+        best = jnp.maximum(best, maxima[pl.ds(tile, items, stride=tiles), :])
     sums = jnp.sum(best, axis=1, keepdims=True) / query_len
     item_down = lax.broadcasted_iota(jnp.int32, (items, LANES), 0)
     item_slot = lax.broadcasted_iota(jnp.int32, (items, LANES), 1)
@@ -326,7 +331,7 @@
     in_hbm = pl.BlockSpec(memory_space=pltpu.HBM)
     pinned = [
         pltpu.with_memory_space_constraint(array, pltpu.HBM)
-        for array in (levels, centroids, resid_words, token_codes, lengths, query_parts[0])
+        for array in (levels, centroids, resid_words.reshape(pass_dev * packed, width), token_codes, lengths, query_parts[0])
     ]
     vmem = pl.BlockSpec(memory_space=pltpu.VMEM)
     tokens = items * plen
@@ -338,13 +343,13 @@
         scratch_shapes=[
             pltpu.VMEM((cent_dev, width), jnp.bfloat16),
             pltpu.VMEM((cent_dev + SUB, width), jnp.float32),
-            pltpu.VMEM((pass_dev, packed, width), jnp.int32),
+            pltpu.VMEM((pass_dev * packed, width), jnp.int32),
             pltpu.VMEM((group_count, group_rows, width), jnp.bfloat16),
             pltpu.VMEM((quads, width, LANES), jnp.bfloat16),
             pltpu.VMEM((width, group_rows), jnp.bfloat16),
             pltpu.VMEM((BLOCKS * SUB * FIELDS, width), jnp.float32),
             pltpu.VMEM((BLOCKS * SUB * FIELDS, width), jnp.bfloat16),
-            pltpu.VMEM((tiles, items + SUB, LANES), jnp.float32),
+            pltpu.VMEM((items * tiles + SUB, LANES), jnp.float32),
             pltpu.VMEM((pass_dev, plen), jnp.int32),
             pltpu.VMEM((SLOTS, BLOCKS * SUB, LANES), jnp.int32),
             pltpu.VMEM((SLOTS, BLOCKS * SUB * FIELDS // LANES, LANES), jnp.int32),
@@ -353,9 +358,6 @@
             pltpu.SMEM((pass_dev,), jnp.int32),
             pltpu.SMEM((work_size,), jnp.int32),
             pltpu.SMEM((work_size // ALIGN + items * tiles // quads,), jnp.int32),
-            pltpu.SMEM((items + 1,), jnp.int32),
-            pltpu.SMEM((items + 1,), jnp.int32),
-            pltpu.SMEM((items + 1,), jnp.int32),
             pltpu.SemaphoreType.DMA((min(quads, PARTS),)),
             pltpu.SemaphoreType.DMA((4,)),
             pltpu.SemaphoreType.DMA((group_count,)),

time: 63 us -> 62.9 us (level)
  Pallas kernels: 29.6 us -> 31.8 us
  blocking collectives: 15.5 us -> 13.3 us
    all_to_all x1, blocking collectives: 15.5 us -> 13.3 us  [shards(): lax.all_to_all(reply, ('cent', 'grp'), split_axis=0, concat_axis=0, tiled...]
    pallas_call x1, Pallas kernels: 26.2 us -> 28.3 us  [owner_scores(): pl.pallas_call(functools.partial(score_kernel, sizes), in_specs=[pl.Block...]
where the time goes in v3:
time: 62.9 us; the launch traced here: 62 us
  Pallas kernels  31.8 us (51%)
  blocking collectives  13.3 us (21%)
  starting transfers between devices  9.22 us (15%)
  waiting for transfers between devices  7.15 us (11%)
  between operations  0.66 us (1%)
    pallas_call x1, Pallas kernels, owner_scores(): pl.pallas_call(functools.partial(score_kernel, sizes), in_specs=[pl.Block...  28.3 us
    all_to_all x1, blocking collectives, shards(): lax.all_to_all(reply, ('cent', 'grp'), split_axis=0, concat_axis=0, tiled...  13.3 us
    all_to_all x1, waiting for transfers between devices, shards(): lax.all_to_all(slots, ('cent', 'grp'), split_axis=0, concat_axis=0, tiled...  7.14 us
    all_to_all x1, starting transfers between devices, shards(): lax.all_to_all(slots, ('cent', 'grp'), split_axis=0, concat_axis=0, tiled...  6.1 us
    ppermute x3, starting transfers between devices, shards(): query_parts.append(lax.ppermute(query_rows, 'grp', pairs))  3.12 us
    pallas_call x1, Pallas kernels, finish(): pl.pallas_call(functools.partial(finish_kernel, sizes), in_specs=[pl.Bloc...  1.91 us
    pallas_call x1, Pallas kernels, slots_by_owner(): pl.pallas_call(functools.partial(slots_kernel, pass_dev, capacity), in_sp...  1.57 us
  transfers between devices with their start and end apart: 4, of which 1 were waited for; matrix products, arithmetic and copies ran while one was open for 0% of the time, Pallas kernels for 3%

profile of v3, /device:TPU:0, one launch (start us, length us, event | category | flops | bytes accessed | tf_op | source)
XLA Modules:
  0.0 62.0 jit_solution(9860032747254920230)
XLA Ops:
  0.6 2.4 %collective-permute-start.2 = (bf16[512,128]{1,0:T(8,128)(2,1)}, bf16[512,128]{1,0:T(8,128)(2,1)S(1)}, u32[]{:S(2)}, u32[]{:S(2)}) collective-permute-start(bf16[512,128]{1,0:T(8,128)(2,1)} %bitcast.12), channel_id=1, source_target_pairs={{0,3},{1,2},{2,1},{3,0},{4,7},{5,6},{6,5},{7,4},{8,11},{9,10},{10,... | collective-permute-start | bytes 393224 | tf_op jit(solution)/shard_map/ppermute | solution.py:431
  3.1 0.6 %collective-permute-start.1 = (bf16[512,128]{1,0:T(8,128)(2,1)}, bf16[512,128]{1,0:T(8,128)(2,1)S(1)}, u32[]{:S(2)}, u32[]{:S(2)}) collective-permute-start(bf16[512,128]{1,0:T(8,128)(2,1)} %bitcast.13), channel_id=1, source_target_pairs={{0,2},{1,3},{2,0},{3,1},{4,6},{5,7},{6,4},{7,5},{8,10},{9,11},{10,... | collective-permute-start | bytes 393224 | tf_op jit(solution)/shard_map/ppermute | solution.py:431
  3.7 0.0 collective-permute-start
  3.8 1.6 %slots_by_owner.1 = (s32[32,8]{1,0:T(8,128)}, s32[1,128]{1,0:T(1,128)}) custom-call(s32[2,64]{1,0:T(2,128)} %bitcast.16), custom_call_target="tpu_custom_call" | custom-call | tf_op jit(solution)/shard_map/slots_by_owner/pallas_call | solution.py:57
  5.3 6.1 %all-to-all-start = ((s32[32,1,8]{2,1,0:T(1,128)}), s32[32,1,8]{2,1,0:T(1,128)S(1)}, u32[]{:S(2)}, u32[]{:S(2)}) async-start(s32[32,1,8]{2,1,0:T(1,128)} %bitcast.10), calls=%async_computation | async-start | bytes 32768 | tf_op jit(solution)/shard_map/all_to_all | solution.py:427
  11.4 7.1 %all-to-all-done = s32[32,1,8]{2,1,0:T(1,128)S(1)} async-done(((s32[32,1,8]{2,1,0:T(1,128)}), s32[32,1,8]{2,1,0:T(1,128)S(1)}, u32[]{:S(2)}, u32[]{:S(2)}) %all-to-all-start) | async-done | bytes 1056 | tf_op jit(solution)/shard_map/all_to_all | solution.py:427
  18.6 0.0 collective-permute-done.2.rest_3_
  18.6 0.0 collective-permute-done.1.rest_2_
  18.6 0.0 collective-permute-done.rest_1_
  18.6 28.3 %owner_scores.1 = f32[32,1,640]{2,1,0:T(1,128)S(1)} custom-call(s32[1]{0:T(128)} %bitcast.me_ref, s32[32,8]{1,0:T(8,128)S(1)} %bitcast.9, f32[4,128]{1,0:T(4,128)} %levels_hbm.1, bf16[32768,128]{1,0:T(8,128)(2,1)} %cent_hbm.1, s32[16384,128]{1,0:T(8,128)} %bitcast.11, s32[512,128]{1,0:T(8,128)} %codes_hbm.1, s32[512]{0:T(512)} %lens_hbm.1, ...), custom_call_target="tpu_custom_call" | custom-call | flops 5368709120 | bytes 16777216 | tf_op jit(solution)/shard_map/owner_scores/pallas_call | solution.py:338
  46.9 13.3 %all_to_all.16.back_ref = f32[32,1,640]{2,1,0:T(1,128)} all-to-all(f32[32,1,640]{2,1,0:T(1,128)S(1)} %owner_scores.1), channel_id=1, replica_groups=mesh['cent'=8,'grp'=4] {'cent','grp'}, dimensions={0} | all-to-all | bytes 163840 | tf_op jit(solution)/shard_map/all_to_all | solution.py:435
  60.1 1.9 %finish.1 = (f32[16,32]{1,0:T(8,128)}, f32[2,64]{1,0:T(2,128)}) custom-call(s32[1]{0:T(128)} %bitcast.me_ref, f32[32,1,640]{2,1,0:T(1,128)} %all_to_all.16.back_ref, s32[1,128]{1,0:T(1,128)} %get-tuple-element.7.target_ref), custom_call_target="tpu_custom_call" | custom-call | tf_op jit(solution)/shard_map/finish/pallas_call | solution.py:401
Async XLA Ops:
  0.6 18.0 %collective-permute-start.2 = (bf16[512,128]{1,0:T(8,128)(2,1)}, bf16[512,128]{1,0:T(8,128)(2,1)S(1)}, u32[]{:S(2)}, u32[]{:S(2)}) collective-permute-start(bf16[512,128]{1,0:T(8,128)(2,1)} %bitcast.12), channel_id=1, source_target_pairs={{0,3},{1,2},{2,1},{3,0},{4,7},{5,6},{6,5},{7,4},{8,11},{9,10},{10,... | collective-permute-start | bytes 393224 | tf_op jit(solution)/shard_map/ppermute | solution.py:431
  3.1 15.5 %collective-permute-start.1 = (bf16[512,128]{1,0:T(8,128)(2,1)}, bf16[512,128]{1,0:T(8,128)(2,1)S(1)}, u32[]{:S(2)}, u32[]{:S(2)}) collective-permute-start(bf16[512,128]{1,0:T(8,128)(2,1)} %bitcast.13), channel_id=1, source_target_pairs={{0,2},{1,3},{2,0},{3,1},{4,6},{5,7},{6,4},{7,5},{8,10},{9,11},{10,... | collective-permute-start | bytes 393224 | tf_op jit(solution)/shard_map/ppermute | solution.py:431
  3.7 14.9 %collective-permute-start = (bf16[512,128]{1,0:T(8,128)(2,1)}, bf16[512,128]{1,0:T(8,128)(2,1)S(1)}, u32[]{:S(2)}, u32[]{:S(2)}) collective-permute-start(bf16[512,128]{1,0:T(8,128)(2,1)} %bitcast.14), channel_id=1, source_target_pairs={{0,1},{1,0},{2,3},{3,2},{4,5},{5,4},{6,7},{7,6},{8,9},{9,8},{10,11... | collective-permute-start | bytes 393224 | tf_op jit(solution)/shard_map/ppermute | solution.py:431
  5.3 13.3 %all-to-all-start = ((s32[32,1,8]{2,1,0:T(1,128)}), s32[32,1,8]{2,1,0:T(1,128)S(1)}, u32[]{:S(2)}, u32[]{:S(2)}) async-start(s32[32,1,8]{2,1,0:T(1,128)} %bitcast.10), calls=%async_computation | async-start | bytes 32768 | tf_op jit(solution)/shard_map/all_to_all | solution.py:427

commit v4 on v3

--- a/solution.py
+++ b/solution.py
@@ -11,9 +11,9 @@
 LANES = 128
 SUB = 8
 FIELDS = 4
-BLOCKS = 16
+BLOCKS = 24
 ALIGN = 4
-SLOTS = 4
+SLOTS = 3
 PARTS = 8
 MIB = 1 << 20
 
@@ -427,8 +427,9 @@
     slots = lax.all_to_all(slots, ("cent", "grp"), split_axis=0, concat_axis=0, tiled=True)
     query_parts = [query_rows]
     for apart in range(1, group_count):
-        pairs = [(index, index ^ apart) for index in range(group_count)]
-        query_parts.append(lax.ppermute(query_rows, "grp", pairs))
+        away, block = (1, query_parts[apart - 1]) if apart % 2 else (apart, query_rows)
+        pairs = [(index, index ^ away) for index in range(group_count)]
+        query_parts.append(lax.ppermute(block, "grp", pairs))
     reply = owner_scores(
         me, slots, query_parts, centroids, token_codes, resid_words, lengths, levels, sizes
     )

time: 62.9 us -> 66.6 us (1.059)
  waiting for transfers between devices: 7.15 us -> 10.8 us
  blocking collectives: 13.3 us -> 9.99 us
  Pallas kernels: 31.8 us -> 34.9 us
    ppermute x3, waiting for transfers between devices: 0.01 us -> 3.71 us  [shards(): query_parts.append(lax.ppermute(block, 'grp', pairs))]
    all_to_all x1, blocking collectives: 13.3 us -> 9.99 us  [shards(): lax.all_to_all(reply, ('cent', 'grp'), split_axis=0, concat_axis=0, tiled...]
    pallas_call x1, Pallas kernels: 28.3 us -> 31.4 us  [owner_scores(): pl.pallas_call(functools.partial(score_kernel, sizes), in_specs=[pl.Block...]
  transfers between devices with their start and end apart: 4 -> 4, of which waited for: 1 -> 2; matrix products, arithmetic and copies ran while one was open for 0% -> 0% of each run, Pallas kernels for 3% -> 2%
where the time goes in v4:
time: 66.6 us; the launch traced here: 65.6 us
  Pallas kernels  34.9 us (52%)
  waiting for transfers between devices  10.8 us (16%)
  blocking collectives  9.99 us (15%)
  starting transfers between devices  9.22 us (14%)
    pallas_call x1, Pallas kernels, owner_scores(): pl.pallas_call(functools.partial(score_kernel, sizes), in_specs=[pl.Block...  31.4 us
    all_to_all x1, blocking collectives, shards(): lax.all_to_all(reply, ('cent', 'grp'), split_axis=0, concat_axis=0, tiled...  9.99 us
    all_to_all x1, waiting for transfers between devices, shards(): lax.all_to_all(slots, ('cent', 'grp'), split_axis=0, concat_axis=0, tiled...  7.14 us
    all_to_all x1, starting transfers between devices, shards(): lax.all_to_all(slots, ('cent', 'grp'), split_axis=0, concat_axis=0, tiled...  6.21 us
    ppermute x3, waiting for transfers between devices, shards(): query_parts.append(lax.ppermute(block, 'grp', pairs))  3.71 us
    ppermute x3, starting transfers between devices, shards(): query_parts.append(lax.ppermute(block, 'grp', pairs))  3.01 us
    pallas_call x1, Pallas kernels, finish(): pl.pallas_call(functools.partial(finish_kernel, sizes), in_specs=[pl.Bloc...  1.91 us
    pallas_call x1, Pallas kernels, slots_by_owner(): pl.pallas_call(functools.partial(slots_kernel, pass_dev, capacity), in_sp...  1.58 us
  transfers between devices with their start and end apart: 4, of which 2 were waited for; matrix products, arithmetic and copies ran while one was open for 0% of the time, Pallas kernels for 2%

profile of v4, /device:TPU:0, one launch (start us, length us, event | category | flops | bytes accessed | tf_op | source)
XLA Modules:
  0.0 65.6 jit_solution(12542387752057376250)
XLA Ops:
  0.6 3.0 %collective-permute-start.1 = (bf16[512,128]{1,0:T(8,128)(2,1)}, bf16[512,128]{1,0:T(8,128)(2,1)S(1)}, u32[]{:S(2)}, u32[]{:S(2)}) collective-permute-start(bf16[512,128]{1,0:T(8,128)(2,1)} %bitcast.12), channel_id=1, source_target_pairs={{0,2},{1,3},{2,0},{3,1},{4,6},{5,7},{6,4},{7,5},{8,10},{9,11},{10,... | collective-permute-start | bytes 393224 | tf_op jit(solution)/shard_map/ppermute | solution.py:432
  3.6 0.0 collective-permute-start
  3.6 3.7 %collective-permute-done.1.rest_2_ = bf16[512,128]{1,0:T(8,128)(2,1)S(1)} collective-permute-done((bf16[512,128]{1,0:T(8,128)(2,1)}, bf16[512,128]{1,0:T(8,128)(2,1)S(1)}, u32[]{:S(2)}, u32[]{:S(2)}) %collective-permute-start.1) | collective-permute-done | bytes 131104 | tf_op jit(solution)/shard_map/ppermute | solution.py:432
  7.3 0.0 collective-permute-start.2
  7.3 1.6 %slots_by_owner.1 = (s32[32,8]{1,0:T(8,128)}, s32[1,128]{1,0:T(1,128)}) custom-call(s32[2,64]{1,0:T(2,128)} %bitcast.15), custom_call_target="tpu_custom_call" | custom-call | tf_op jit(solution)/shard_map/slots_by_owner/pallas_call | solution.py:57
  8.9 6.2 %all-to-all-start = ((s32[32,1,8]{2,1,0:T(1,128)}), s32[32,1,8]{2,1,0:T(1,128)S(1)}, u32[]{:S(2)}, u32[]{:S(2)}) async-start(s32[32,1,8]{2,1,0:T(1,128)} %bitcast.10), calls=%async_computation | async-start | bytes 32768 | tf_op jit(solution)/shard_map/all_to_all | solution.py:427
  15.1 7.1 %all-to-all-done = s32[32,1,8]{2,1,0:T(1,128)S(1)} async-done(((s32[32,1,8]{2,1,0:T(1,128)}), s32[32,1,8]{2,1,0:T(1,128)S(1)}, u32[]{:S(2)}, u32[]{:S(2)}) %all-to-all-start) | async-done | bytes 1056 | tf_op jit(solution)/shard_map/all_to_all | solution.py:427
  22.3 0.0 collective-permute-done.rest_1_
  22.3 0.0 collective-permute-done.2.rest_3_
  22.3 31.4 %owner_scores.1 = f32[32,1,640]{2,1,0:T(1,128)S(1)} custom-call(s32[1]{0:T(128)} %bitcast.me_ref, s32[32,8]{1,0:T(8,128)S(1)} %bitcast.9, f32[4,128]{1,0:T(4,128)} %levels_hbm.1, bf16[32768,128]{1,0:T(8,128)(2,1)} %cent_hbm.1, s32[16384,128]{1,0:T(8,128)} %bitcast.11, s32[512,128]{1,0:T(8,128)} %codes_hbm.1, s32[512]{0:T(512)} %lens_hbm.1, ...), custom_call_target="tpu_custom_call" | custom-call | flops 5368709120 | bytes 16777216 | tf_op jit(solution)/shard_map/owner_scores/pallas_call | solution.py:338
  53.7 10.0 %all_to_all.16.back_ref = f32[32,1,640]{2,1,0:T(1,128)} all-to-all(f32[32,1,640]{2,1,0:T(1,128)S(1)} %owner_scores.1), channel_id=1, replica_groups=mesh['cent'=8,'grp'=4] {'cent','grp'}, dimensions={0} | all-to-all | bytes 163840 | tf_op jit(solution)/shard_map/all_to_all | solution.py:436
  63.7 1.9 %finish.1 = (f32[16,32]{1,0:T(8,128)}, f32[2,64]{1,0:T(2,128)}) custom-call(s32[1]{0:T(128)} %bitcast.me_ref, f32[32,1,640]{2,1,0:T(1,128)} %all_to_all.16.back_ref, s32[1,128]{1,0:T(1,128)} %get-tuple-element.7.target_ref), custom_call_target="tpu_custom_call" | custom-call | tf_op jit(solution)/shard_map/finish/pallas_call | solution.py:401
Async XLA Ops:
  0.6 6.7 %collective-permute-start.1 = (bf16[512,128]{1,0:T(8,128)(2,1)}, bf16[512,128]{1,0:T(8,128)(2,1)S(1)}, u32[]{:S(2)}, u32[]{:S(2)}) collective-permute-start(bf16[512,128]{1,0:T(8,128)(2,1)} %bitcast.12), channel_id=1, source_target_pairs={{0,2},{1,3},{2,0},{3,1},{4,6},{5,7},{6,4},{7,5},{8,10},{9,11},{10,... | collective-permute-start | bytes 393224 | tf_op jit(solution)/shard_map/ppermute | solution.py:432
  3.6 18.7 %collective-permute-start = (bf16[512,128]{1,0:T(8,128)(2,1)}, bf16[512,128]{1,0:T(8,128)(2,1)S(1)}, u32[]{:S(2)}, u32[]{:S(2)}) collective-permute-start(bf16[512,128]{1,0:T(8,128)(2,1)} %bitcast.13), channel_id=1, source_target_pairs={{0,1},{1,0},{2,3},{3,2},{4,5},{5,4},{6,7},{7,6},{8,9},{9,8},{10,11... | collective-permute-start | bytes 393224 | tf_op jit(solution)/shard_map/ppermute | solution.py:432
  7.3 14.9 %collective-permute-start.2 = (bf16[512,128]{1,0:T(8,128)(2,1)S(1)}, bf16[512,128]{1,0:T(8,128)(2,1)S(1)}, u32[]{:S(2)}, u32[]{:S(2)}) collective-permute-start(bf16[512,128]{1,0:T(8,128)(2,1)S(1)} %collective-permute-done.1.rest_2_), channel_id=1, source_target_pairs={{0,1},{1,0},{2,3},{3,2},{4,5},{5,4},{6,7},{7,6},{8,9},{9,8},{10,11... | collective-permute-start | bytes 393224 | tf_op jit(solution)/shard_map/ppermute | solution.py:432
  8.9 13.4 %all-to-all-start = ((s32[32,1,8]{2,1,0:T(1,128)}), s32[32,1,8]{2,1,0:T(1,128)S(1)}, u32[]{:S(2)}, u32[]{:S(2)}) async-start(s32[32,1,8]{2,1,0:T(1,128)} %bitcast.10), calls=%async_computation | async-start | bytes 32768 | tf_op jit(solution)/shard_map/all_to_all | solution.py:427

commit v5 on v3

--- a/solution.py
+++ b/solution.py
@@ -62,6 +62,7 @@
             jax.ShapeDtypeStruct((devices, capacity), jnp.int32),
             jax.ShapeDtypeStruct((1, cand.size), jnp.int32),
         ],
+        compiler_params=pltpu.CompilerParams(vmem_limit_bytes=4 * MIB),
         name="slots_by_owner",
     )(cand)
 
@@ -406,6 +407,7 @@
             jax.ShapeDtypeStruct((group_rows, query_len), jnp.float32),
             jax.ShapeDtypeStruct((per_device, cand_count), jnp.float32),
         ],
+        compiler_params=pltpu.CompilerParams(vmem_limit_bytes=4 * MIB),
         name="finish",
     )(me, back, target)
 

time: 62.9 us -> 62 us (0.986); the launches traced: 62 us -> 62.1 us
  Pallas kernels: 31.8 us -> 22.8 us
  blocking collectives: 13.3 us -> 21.6 us
  local copies, waits for them, and re-layouts: 0 us -> 0.68 us
    all_to_all x1, blocking collectives: 13.3 us -> 21.6 us  [shards(): lax.all_to_all(reply, ('cent', 'grp'), split_axis=0, concat_axis=0, tiled...]
    pallas_call x1, Pallas kernels: 28.3 us -> 20.9 us  [owner_scores(): pl.pallas_call(functools.partial(score_kernel, sizes), in_specs=[pl.Block...]
    pallas_call x1, Pallas kernels: 1.91 us -> 1.02 us  [finish(): pl.pallas_call(functools.partial(finish_kernel, sizes), in_specs=[pl.Bloc...]
    pallas_call x1, Pallas kernels: 1.57 us -> 0.89 us  [slots_by_owner(): pl.pallas_call(functools.partial(slots_kernel, pass_dev, capacity), in_sp...]
    unnamed x0 -> x2, local copies, waits for them, and re-layouts: none -> 0.68 us
  transfers between devices with their start and end apart: 4 -> 4, of which waited for: 1 -> 1; matrix products, arithmetic and copies ran while one was open for 0% -> 0% of each run, Pallas kernels for 3% -> 1%
where the time goes in v5:
time: 62 us; the launch traced here: 62.1 us
  Pallas kernels  22.8 us (37%)
  blocking collectives  21.6 us (35%)
  starting transfers between devices  9.22 us (15%)
  waiting for transfers between devices  7.15 us (12%)
  local copies, waits for them, and re-layouts  0.68 us (1%)
  between operations  0.66 us (1%)
    all_to_all x1, blocking collectives, shards(): lax.all_to_all(reply, ('cent', 'grp'), split_axis=0, concat_axis=0, tiled...  21.6 us
    pallas_call x1, Pallas kernels, owner_scores(): pl.pallas_call(functools.partial(score_kernel, sizes), in_specs=[pl.Block...  20.9 us
    all_to_all x1, waiting for transfers between devices, shards(): lax.all_to_all(slots, ('cent', 'grp'), split_axis=0, concat_axis=0, tiled...  7.14 us
    all_to_all x1, starting transfers between devices, shards(): lax.all_to_all(slots, ('cent', 'grp'), split_axis=0, concat_axis=0, tiled...  6.1 us
    ppermute x3, starting transfers between devices, shards(): query_parts.append(lax.ppermute(query_rows, 'grp', pairs))  3.12 us
  transfers between devices with their start and end apart: 4, of which 1 were waited for; matrix products, arithmetic and copies ran while one was open for 0% of the time, Pallas kernels for 1%

profile of v5, /device:TPU:0, one launch (start us, length us, event | category | flops | bytes accessed | tf_op | source)
XLA Modules:
  0.0 62.1 jit_solution(4600484016035699314)
XLA Ops:
  0.6 2.4 %collective-permute-start.2 = (bf16[512,128]{1,0:T(8,128)(2,1)}, bf16[512,128]{1,0:T(8,128)(2,1)S(1)}, u32[]{:S(2)}, u32[]{:S(2)}) collective-permute-start(bf16[512,128]{1,0:T(8,128)(2,1)} %bitcast.12), channel_id=1, source_target_pairs={{0,3},{1,2},{2,1},{3,0},{4,7},{5,6},{6,5},{7,4},{8,11},{9,10},{10,... | collective-permute-start | bytes 393224 | tf_op jit(solution)/shard_map/ppermute | solution.py:433
  3.1 0.6 %collective-permute-start.1 = (bf16[512,128]{1,0:T(8,128)(2,1)}, bf16[512,128]{1,0:T(8,128)(2,1)S(1)}, u32[]{:S(2)}, u32[]{:S(2)}) collective-permute-start(bf16[512,128]{1,0:T(8,128)(2,1)} %bitcast.13), channel_id=1, source_target_pairs={{0,2},{1,3},{2,0},{3,1},{4,6},{5,7},{6,4},{7,5},{8,10},{9,11},{10,... | collective-permute-start | bytes 393224 | tf_op jit(solution)/shard_map/ppermute | solution.py:433
  3.7 0.0 collective-permute-start
  3.8 0.0 copy-start
  3.8 0.7 %copy-done = s32[1,1,2,64]{3,2,1,0:T(2,128)S(1)} copy-done((s32[1,1,2,64]{3,2,1,0:T(2,128)S(1)}, s32[1,1,2,64]{3,2,1,0:T(2,128)}, u32[]{:S(2)}) %copy-start) | copy-done | bytes 536
  4.4 0.9 %slots_by_owner.1 = (s32[32,8]{1,0:T(8,128)}, s32[1,128]{1,0:T(1,128)S(1)}) custom-call(s32[2,64]{1,0:T(2,128)S(1)} %bitcast.10), custom_call_target="tpu_custom_call" | custom-call | tf_op jit(solution)/shard_map/slots_by_owner/pallas_call | solution.py:57
  5.3 6.1 %all-to-all-start = ((s32[32,1,8]{2,1,0:T(1,128)}), s32[32,1,8]{2,1,0:T(1,128)S(1)}, u32[]{:S(2)}, u32[]{:S(2)}) async-start(s32[32,1,8]{2,1,0:T(1,128)} %bitcast.3), calls=%async_computation | async-start | bytes 32768 | tf_op jit(solution)/shard_map/all_to_all | solution.py:429
  11.4 7.1 %all-to-all-done = s32[32,1,8]{2,1,0:T(1,128)S(1)} async-done(((s32[32,1,8]{2,1,0:T(1,128)}), s32[32,1,8]{2,1,0:T(1,128)S(1)}, u32[]{:S(2)}, u32[]{:S(2)}) %all-to-all-start) | async-done | bytes 1056 | tf_op jit(solution)/shard_map/all_to_all | solution.py:429
  18.6 0.0 collective-permute-done.2.rest_3_
  18.6 0.0 collective-permute-done.1.rest_2_
  18.6 0.0 collective-permute-done.rest_1_
  18.6 20.9 %owner_scores.1 = f32[32,1,640]{2,1,0:T(1,128)S(1)} custom-call(s32[1]{0:T(128)} %bitcast.me_ref, s32[32,8]{1,0:T(8,128)S(1)} %bitcast.9, f32[4,128]{1,0:T(4,128)} %levels_hbm.1, bf16[32768,128]{1,0:T(8,128)(2,1)} %cent_hbm.1, s32[16384,128]{1,0:T(8,128)} %bitcast.11, s32[512,128]{1,0:T(8,128)} %codes_hbm.1, s32[512]{0:T(512)} %lens_hbm.1, ...), custom_call_target="tpu_custom_call" | custom-call | flops 5368709120 | bytes 16777216 | tf_op jit(solution)/shard_map/owner_scores/pallas_call | solution.py:339
  39.5 21.6 %all_to_all.16.back_ref = f32[32,1,640]{2,1,0:T(1,128)S(1)} all-to-all(f32[32,1,640]{2,1,0:T(1,128)S(1)} %owner_scores.1), channel_id=1, replica_groups=mesh['cent'=8,'grp'=4] {'cent','grp'}, dimensions={0} | all-to-all | bytes 163840 | tf_op jit(solution)/shard_map/all_to_all | solution.py:437
  61.1 1.0 %finish.1 = (f32[16,32]{1,0:T(8,128)}, f32[2,64]{1,0:T(2,128)}) custom-call(s32[1]{0:T(128)} %bitcast.me_ref, f32[32,1,640]{2,1,0:T(1,128)S(1)} %all_to_all.16.back_ref, s32[1,128]{1,0:T(1,128)S(1)} %get-tuple-element.7.target_ref), custom_call_target="tpu_custom_call" | custom-call | tf_op jit(solution)/shard_map/finish/pallas_call | solution.py:402
Async XLA Ops:
  0.6 18.0 %collective-permute-start.2 = (bf16[512,128]{1,0:T(8,128)(2,1)}, bf16[512,128]{1,0:T(8,128)(2,1)S(1)}, u32[]{:S(2)}, u32[]{:S(2)}) collective-permute-start(bf16[512,128]{1,0:T(8,128)(2,1)} %bitcast.12), channel_id=1, source_target_pairs={{0,3},{1,2},{2,1},{3,0},{4,7},{5,6},{6,5},{7,4},{8,11},{9,10},{10,... | collective-permute-start | bytes 393224 | tf_op jit(solution)/shard_map/ppermute | solution.py:433
  3.1 15.5 %collective-permute-start.1 = (bf16[512,128]{1,0:T(8,128)(2,1)}, bf16[512,128]{1,0:T(8,128)(2,1)S(1)}, u32[]{:S(2)}, u32[]{:S(2)}) collective-permute-start(bf16[512,128]{1,0:T(8,128)(2,1)} %bitcast.13), channel_id=1, source_target_pairs={{0,2},{1,3},{2,0},{3,1},{4,6},{5,7},{6,4},{7,5},{8,10},{9,11},{10,... | collective-permute-start | bytes 393224 | tf_op jit(solution)/shard_map/ppermute | solution.py:433
  3.7 14.9 %collective-permute-start = (bf16[512,128]{1,0:T(8,128)(2,1)}, bf16[512,128]{1,0:T(8,128)(2,1)S(1)}, u32[]{:S(2)}, u32[]{:S(2)}) collective-permute-start(bf16[512,128]{1,0:T(8,128)(2,1)} %bitcast.14), channel_id=1, source_target_pairs={{0,1},{1,0},{2,3},{3,2},{4,5},{5,4},{6,7},{7,6},{8,9},{9,8},{10,11... | collective-permute-start | bytes 393224 | tf_op jit(solution)/shard_map/ppermute | solution.py:433
  3.8 0.7 %copy-start = (s32[1,1,2,64]{3,2,1,0:T(2,128)S(1)}, s32[1,1,2,64]{3,2,1,0:T(2,128)}, u32[]{:S(2)}) copy-start(s32[1,1,2,64]{3,2,1,0:T(2,128)} %param.9) | copy-start | bytes 1540
  5.3 13.3 %all-to-all-start = ((s32[32,1,8]{2,1,0:T(1,128)}), s32[32,1,8]{2,1,0:T(1,128)S(1)}, u32[]{:S(2)}, u32[]{:S(2)}) async-start(s32[32,1,8]{2,1,0:T(1,128)} %bitcast.3), calls=%async_computation | async-start | bytes 32768 | tf_op jit(solution)/shard_map/all_to_all | solution.py:429

commit v6 on v5

--- a/solution.py
+++ b/solution.py
@@ -187,7 +187,7 @@
     lowest = jnp.full((SUB, own_t.shape[1]), -jnp.inf, jnp.float32)
     total, token_best = lax.fori_loop(0, parts, prepare, (0, lowest))
     token_best = jnp.max(token_best, axis=0, keepdims=True)
-    for index in range((SLOTS + 1) * BLOCKS):
+    for index in range((SLOTS + 2) * BLOCKS):
         work[total + index] = spare
     for index in range(2 * BLOCKS // ALIGN):
         work_quad[total // ALIGN + index] = 0
@@ -276,6 +276,10 @@
         elif slot < SLOTS - 1:
             pl.when(slot < chunks)(slot_copy(slot).start)
 
+    best_lanes = token_best.shape[1]
+    for source in range(sources):
+        out_ref[source, :, :best_lanes] = token_best
+
     def step(group, carry):
         for slot in range(SLOTS):
             chunk = SLOTS * group + slot
@@ -310,9 +314,7 @@
     by_source = jnp.dot(
         gather, spread, precision=lax.Precision.HIGHEST, preferred_element_type=jnp.float32
     )
-    best_lanes = token_best.shape[1]
     for source in range(sources):
-        out_ref[source, :, :best_lanes] = token_best
         out_ref[source, :, best_lanes:] = by_source[source : source + 1, :]
 
 
@@ -327,7 +329,7 @@
     tiles = packed // SUB
     items = sources * capacity
     quads = group_count * group_rows // LANES
-    work_size = items * tiles + quads * ALIGN + (SLOTS + 1) * BLOCKS
+    work_size = items * tiles + quads * ALIGN + (SLOTS + 2) * BLOCKS
     any_space = pl.BlockSpec(memory_space=pl.ANY)
     in_hbm = pl.BlockSpec(memory_space=pltpu.HBM)
     pinned = [

time: 62 us -> 61.9 us (level); the launches traced: 62.1 us -> 61.2 us
  blocking collectives: 21.6 us -> 20.2 us
    all_to_all x1, blocking collectives: 21.6 us -> 20.2 us  [shards(): lax.all_to_all(reply, ('cent', 'grp'), split_axis=0, concat_axis=0, tiled...]
where the time goes in v6:
time: 61.9 us; the launch traced here: 61.2 us
  Pallas kernels  23.3 us (38%)
  blocking collectives  20.2 us (33%)
  starting transfers between devices  9.22 us (15%)
  waiting for transfers between devices  7.15 us (12%)
  local copies, waits for them, and re-layouts  0.68 us (1%)
  between operations  0.66 us (1%)
    pallas_call x1, Pallas kernels, owner_scores(): pl.pallas_call(functools.partial(score_kernel, sizes), in_specs=[pl.Block...  21.4 us
    all_to_all x1, blocking collectives, shards(): lax.all_to_all(reply, ('cent', 'grp'), split_axis=0, concat_axis=0, tiled...  20.2 us
    all_to_all x1, waiting for transfers between devices, shards(): lax.all_to_all(slots, ('cent', 'grp'), split_axis=0, concat_axis=0, tiled...  7.14 us
    all_to_all x1, starting transfers between devices, shards(): lax.all_to_all(slots, ('cent', 'grp'), split_axis=0, concat_axis=0, tiled...  6.1 us
    ppermute x3, starting transfers between devices, shards(): query_parts.append(lax.ppermute(query_rows, 'grp', pairs))  3.12 us
  transfers between devices with their start and end apart: 4, of which 1 were waited for; matrix products, arithmetic and copies ran while one was open for 0% of the time, Pallas kernels for 1%

profile of v6, /device:TPU:0, one launch (start us, length us, event | category | flops | bytes accessed | tf_op | source)
XLA Modules:
  0.0 61.2 jit_solution(11514640373580857317)
XLA Ops:
  0.6 2.4 %collective-permute-start.2 = (bf16[512,128]{1,0:T(8,128)(2,1)}, bf16[512,128]{1,0:T(8,128)(2,1)S(1)}, u32[]{:S(2)}, u32[]{:S(2)}) collective-permute-start(bf16[512,128]{1,0:T(8,128)(2,1)} %bitcast.12), channel_id=1, source_target_pairs={{0,3},{1,2},{2,1},{3,0},{4,7},{5,6},{6,5},{7,4},{8,11},{9,10},{10,... | collective-permute-start | bytes 393224 | tf_op jit(solution)/shard_map/ppermute | solution.py:435
  3.1 0.6 %collective-permute-start.1 = (bf16[512,128]{1,0:T(8,128)(2,1)}, bf16[512,128]{1,0:T(8,128)(2,1)S(1)}, u32[]{:S(2)}, u32[]{:S(2)}) collective-permute-start(bf16[512,128]{1,0:T(8,128)(2,1)} %bitcast.13), channel_id=1, source_target_pairs={{0,2},{1,3},{2,0},{3,1},{4,6},{5,7},{6,4},{7,5},{8,10},{9,11},{10,... | collective-permute-start | bytes 393224 | tf_op jit(solution)/shard_map/ppermute | solution.py:435
  3.7 0.0 collective-permute-start
  3.8 0.0 copy-start
  3.8 0.7 %copy-done = s32[1,1,2,64]{3,2,1,0:T(2,128)S(1)} copy-done((s32[1,1,2,64]{3,2,1,0:T(2,128)S(1)}, s32[1,1,2,64]{3,2,1,0:T(2,128)}, u32[]{:S(2)}) %copy-start) | copy-done | bytes 536
  4.4 0.9 %slots_by_owner.1 = (s32[32,8]{1,0:T(8,128)}, s32[1,128]{1,0:T(1,128)S(1)}) custom-call(s32[2,64]{1,0:T(2,128)S(1)} %bitcast.10), custom_call_target="tpu_custom_call" | custom-call | tf_op jit(solution)/shard_map/slots_by_owner/pallas_call | solution.py:57
  5.3 6.1 %all-to-all-start = ((s32[32,1,8]{2,1,0:T(1,128)}), s32[32,1,8]{2,1,0:T(1,128)S(1)}, u32[]{:S(2)}, u32[]{:S(2)}) async-start(s32[32,1,8]{2,1,0:T(1,128)} %bitcast.3), calls=%async_computation | async-start | bytes 32768 | tf_op jit(solution)/shard_map/all_to_all | solution.py:431
  11.4 7.1 %all-to-all-done = s32[32,1,8]{2,1,0:T(1,128)S(1)} async-done(((s32[32,1,8]{2,1,0:T(1,128)}), s32[32,1,8]{2,1,0:T(1,128)S(1)}, u32[]{:S(2)}, u32[]{:S(2)}) %all-to-all-start) | async-done | bytes 1056 | tf_op jit(solution)/shard_map/all_to_all | solution.py:431
  18.6 0.0 collective-permute-done.2.rest_3_
  18.6 0.0 collective-permute-done.1.rest_2_
  18.6 0.0 collective-permute-done.rest_1_
  18.6 21.4 %owner_scores.1 = f32[32,1,640]{2,1,0:T(1,128)S(1)} custom-call(s32[1]{0:T(128)} %bitcast.me_ref, s32[32,8]{1,0:T(8,128)S(1)} %bitcast.9, f32[4,128]{1,0:T(4,128)} %levels_hbm.1, bf16[32768,128]{1,0:T(8,128)(2,1)} %cent_hbm.1, s32[16384,128]{1,0:T(8,128)} %bitcast.11, s32[512,128]{1,0:T(8,128)} %codes_hbm.1, s32[512]{0:T(512)} %lens_hbm.1, ...), custom_call_target="tpu_custom_call" | custom-call | flops 5368709120 | bytes 16777216 | tf_op jit(solution)/shard_map/owner_scores/pallas_call | solution.py:341
  40.0 20.2 %all_to_all.16.back_ref = f32[32,1,640]{2,1,0:T(1,128)S(1)} all-to-all(f32[32,1,640]{2,1,0:T(1,128)S(1)} %owner_scores.1), channel_id=1, replica_groups=mesh['cent'=8,'grp'=4] {'cent','grp'}, dimensions={0} | all-to-all | bytes 163840 | tf_op jit(solution)/shard_map/all_to_all | solution.py:439
  60.2 1.0 %finish.1 = (f32[16,32]{1,0:T(8,128)}, f32[2,64]{1,0:T(2,128)}) custom-call(s32[1]{0:T(128)} %bitcast.me_ref, f32[32,1,640]{2,1,0:T(1,128)S(1)} %all_to_all.16.back_ref, s32[1,128]{1,0:T(1,128)S(1)} %get-tuple-element.7.target_ref), custom_call_target="tpu_custom_call" | custom-call | tf_op jit(solution)/shard_map/finish/pallas_call | solution.py:404
Async XLA Ops:
  0.6 18.0 %collective-permute-start.2 = (bf16[512,128]{1,0:T(8,128)(2,1)}, bf16[512,128]{1,0:T(8,128)(2,1)S(1)}, u32[]{:S(2)}, u32[]{:S(2)}) collective-permute-start(bf16[512,128]{1,0:T(8,128)(2,1)} %bitcast.12), channel_id=1, source_target_pairs={{0,3},{1,2},{2,1},{3,0},{4,7},{5,6},{6,5},{7,4},{8,11},{9,10},{10,... | collective-permute-start | bytes 393224 | tf_op jit(solution)/shard_map/ppermute | solution.py:435
  3.1 15.5 %collective-permute-start.1 = (bf16[512,128]{1,0:T(8,128)(2,1)}, bf16[512,128]{1,0:T(8,128)(2,1)S(1)}, u32[]{:S(2)}, u32[]{:S(2)}) collective-permute-start(bf16[512,128]{1,0:T(8,128)(2,1)} %bitcast.13), channel_id=1, source_target_pairs={{0,2},{1,3},{2,0},{3,1},{4,6},{5,7},{6,4},{7,5},{8,10},{9,11},{10,... | collective-permute-start | bytes 393224 | tf_op jit(solution)/shard_map/ppermute | solution.py:435
  3.7 14.9 %collective-permute-start = (bf16[512,128]{1,0:T(8,128)(2,1)}, bf16[512,128]{1,0:T(8,128)(2,1)S(1)}, u32[]{:S(2)}, u32[]{:S(2)}) collective-permute-start(bf16[512,128]{1,0:T(8,128)(2,1)} %bitcast.14), channel_id=1, source_target_pairs={{0,1},{1,0},{2,3},{3,2},{4,5},{5,4},{6,7},{7,6},{8,9},{9,8},{10,11... | collective-permute-start | bytes 393224 | tf_op jit(solution)/shard_map/ppermute | solution.py:435
  3.8 0.7 %copy-start = (s32[1,1,2,64]{3,2,1,0:T(2,128)S(1)}, s32[1,1,2,64]{3,2,1,0:T(2,128)}, u32[]{:S(2)}) copy-start(s32[1,1,2,64]{3,2,1,0:T(2,128)} %param.9) | copy-start | bytes 1540
  5.3 13.3 %all-to-all-start = ((s32[32,1,8]{2,1,0:T(1,128)}), s32[32,1,8]{2,1,0:T(1,128)S(1)}, u32[]{:S(2)}, u32[]{:S(2)}) async-start(s32[32,1,8]{2,1,0:T(1,128)} %bitcast.3), calls=%async_computation | async-start | bytes 32768 | tf_op jit(solution)/shard_map/all_to_all | solution.py:431

commit v7 on v6

--- a/solution.py
+++ b/solution.py
@@ -14,7 +14,7 @@
 BLOCKS = 16
 ALIGN = 4
 SLOTS = 4
-PARTS = 8
+PARTS = 4
 MIB = 1 << 20
 
 

time: 61.9 us -> 62.4 us (level); the launches traced: 61.2 us -> 62.5 us
  Pallas kernels: 23.3 us -> 25.2 us
  blocking collectives: 20.2 us -> 19.5 us
    pallas_call x1, Pallas kernels: 21.4 us -> 23.3 us  [owner_scores(): pl.pallas_call(functools.partial(score_kernel, sizes), in_specs=[pl.Block...]
    all_to_all x1, blocking collectives: 20.2 us -> 19.5 us  [shards(): lax.all_to_all(reply, ('cent', 'grp'), split_axis=0, concat_axis=0, tiled...]
where the time goes in v7:
time: 62.4 us; the launch traced here: 62.5 us
  Pallas kernels  25.2 us (40%)
  blocking collectives  19.5 us (31%)
  starting transfers between devices  9.22 us (15%)
  waiting for transfers between devices  7.15 us (11%)
  local copies, waits for them, and re-layouts  0.68 us (1%)
  between operations  0.66 us (1%)
    pallas_call x1, Pallas kernels, owner_scores(): pl.pallas_call(functools.partial(score_kernel, sizes), in_specs=[pl.Block...  23.3 us
    all_to_all x1, blocking collectives, shards(): lax.all_to_all(reply, ('cent', 'grp'), split_axis=0, concat_axis=0, tiled...  19.5 us
    all_to_all x1, waiting for transfers between devices, shards(): lax.all_to_all(slots, ('cent', 'grp'), split_axis=0, concat_axis=0, tiled...  7.14 us
    all_to_all x1, starting transfers between devices, shards(): lax.all_to_all(slots, ('cent', 'grp'), split_axis=0, concat_axis=0, tiled...  6.1 us
    ppermute x3, starting transfers between devices, shards(): query_parts.append(lax.ppermute(query_rows, 'grp', pairs))  3.12 us
  transfers between devices with their start and end apart: 4, of which 1 were waited for; matrix products, arithmetic and copies ran while one was open for 0% of the time, Pallas kernels for 1%

profile of v7, /device:TPU:0, one launch (start us, length us, event | category | flops | bytes accessed | tf_op | source)
XLA Modules:
  0.0 62.5 jit_solution(8721580076762343927)
XLA Ops:
  0.6 2.4 %collective-permute-start.2 = (bf16[512,128]{1,0:T(8,128)(2,1)}, bf16[512,128]{1,0:T(8,128)(2,1)S(1)}, u32[]{:S(2)}, u32[]{:S(2)}) collective-permute-start(bf16[512,128]{1,0:T(8,128)(2,1)} %bitcast.12), channel_id=1, source_target_pairs={{0,3},{1,2},{2,1},{3,0},{4,7},{5,6},{6,5},{7,4},{8,11},{9,10},{10,... | collective-permute-start | bytes 393224 | tf_op jit(solution)/shard_map/ppermute | solution.py:435
  3.1 0.6 %collective-permute-start.1 = (bf16[512,128]{1,0:T(8,128)(2,1)}, bf16[512,128]{1,0:T(8,128)(2,1)S(1)}, u32[]{:S(2)}, u32[]{:S(2)}) collective-permute-start(bf16[512,128]{1,0:T(8,128)(2,1)} %bitcast.13), channel_id=1, source_target_pairs={{0,2},{1,3},{2,0},{3,1},{4,6},{5,7},{6,4},{7,5},{8,10},{9,11},{10,... | collective-permute-start | bytes 393224 | tf_op jit(solution)/shard_map/ppermute | solution.py:435
  3.7 0.0 collective-permute-start
  3.8 0.0 copy-start
  3.8 0.7 %copy-done = s32[1,1,2,64]{3,2,1,0:T(2,128)S(1)} copy-done((s32[1,1,2,64]{3,2,1,0:T(2,128)S(1)}, s32[1,1,2,64]{3,2,1,0:T(2,128)}, u32[]{:S(2)}) %copy-start) | copy-done | bytes 536
  4.4 0.9 %slots_by_owner.1 = (s32[32,8]{1,0:T(8,128)}, s32[1,128]{1,0:T(1,128)S(1)}) custom-call(s32[2,64]{1,0:T(2,128)S(1)} %bitcast.10), custom_call_target="tpu_custom_call" | custom-call | tf_op jit(solution)/shard_map/slots_by_owner/pallas_call | solution.py:57
  5.3 6.1 %all-to-all-start = ((s32[32,1,8]{2,1,0:T(1,128)}), s32[32,1,8]{2,1,0:T(1,128)S(1)}, u32[]{:S(2)}, u32[]{:S(2)}) async-start(s32[32,1,8]{2,1,0:T(1,128)} %bitcast.3), calls=%async_computation | async-start | bytes 32768 | tf_op jit(solution)/shard_map/all_to_all | solution.py:431
  11.4 7.1 %all-to-all-done = s32[32,1,8]{2,1,0:T(1,128)S(1)} async-done(((s32[32,1,8]{2,1,0:T(1,128)}), s32[32,1,8]{2,1,0:T(1,128)S(1)}, u32[]{:S(2)}, u32[]{:S(2)}) %all-to-all-start) | async-done | bytes 1056 | tf_op jit(solution)/shard_map/all_to_all | solution.py:431
  18.6 0.0 collective-permute-done.2.rest_3_
  18.6 0.0 collective-permute-done.1.rest_2_
  18.6 0.0 collective-permute-done.rest_1_
  18.6 23.3 %owner_scores.1 = f32[32,1,640]{2,1,0:T(1,128)S(1)} custom-call(s32[1]{0:T(128)} %bitcast.me_ref, s32[32,8]{1,0:T(8,128)S(1)} %bitcast.9, f32[4,128]{1,0:T(4,128)} %levels_hbm.1, bf16[32768,128]{1,0:T(8,128)(2,1)} %cent_hbm.1, s32[16384,128]{1,0:T(8,128)} %bitcast.11, s32[512,128]{1,0:T(8,128)} %codes_hbm.1, s32[512]{0:T(512)} %lens_hbm.1, ...), custom_call_target="tpu_custom_call" | custom-call | flops 5368709120 | bytes 16777216 | tf_op jit(solution)/shard_map/owner_scores/pallas_call | solution.py:341
  41.9 19.5 %all_to_all.16.back_ref = f32[32,1,640]{2,1,0:T(1,128)S(1)} all-to-all(f32[32,1,640]{2,1,0:T(1,128)S(1)} %owner_scores.1), channel_id=1, replica_groups=mesh['cent'=8,'grp'=4] {'cent','grp'}, dimensions={0} | all-to-all | bytes 163840 | tf_op jit(solution)/shard_map/all_to_all | solution.py:439
  61.4 1.0 %finish.1 = (f32[16,32]{1,0:T(8,128)}, f32[2,64]{1,0:T(2,128)}) custom-call(s32[1]{0:T(128)} %bitcast.me_ref, f32[32,1,640]{2,1,0:T(1,128)S(1)} %all_to_all.16.back_ref, s32[1,128]{1,0:T(1,128)S(1)} %get-tuple-element.7.target_ref), custom_call_target="tpu_custom_call" | custom-call | tf_op jit(solution)/shard_map/finish/pallas_call | solution.py:404
Async XLA Ops:
  0.6 18.0 %collective-permute-start.2 = (bf16[512,128]{1,0:T(8,128)(2,1)}, bf16[512,128]{1,0:T(8,128)(2,1)S(1)}, u32[]{:S(2)}, u32[]{:S(2)}) collective-permute-start(bf16[512,128]{1,0:T(8,128)(2,1)} %bitcast.12), channel_id=1, source_target_pairs={{0,3},{1,2},{2,1},{3,0},{4,7},{5,6},{6,5},{7,4},{8,11},{9,10},{10,... | collective-permute-start | bytes 393224 | tf_op jit(solution)/shard_map/ppermute | solution.py:435
  3.1 15.5 %collective-permute-start.1 = (bf16[512,128]{1,0:T(8,128)(2,1)}, bf16[512,128]{1,0:T(8,128)(2,1)S(1)}, u32[]{:S(2)}, u32[]{:S(2)}) collective-permute-start(bf16[512,128]{1,0:T(8,128)(2,1)} %bitcast.13), channel_id=1, source_target_pairs={{0,2},{1,3},{2,0},{3,1},{4,6},{5,7},{6,4},{7,5},{8,10},{9,11},{10,... | collective-permute-start | bytes 393224 | tf_op jit(solution)/shard_map/ppermute | solution.py:435
  3.7 14.9 %collective-permute-start = (bf16[512,128]{1,0:T(8,128)(2,1)}, bf16[512,128]{1,0:T(8,128)(2,1)S(1)}, u32[]{:S(2)}, u32[]{:S(2)}) collective-permute-start(bf16[512,128]{1,0:T(8,128)(2,1)} %bitcast.14), channel_id=1, source_target_pairs={{0,1},{1,0},{2,3},{3,2},{4,5},{5,4},{6,7},{7,6},{8,9},{9,8},{10,11... | collective-permute-start | bytes 393224 | tf_op jit(solution)/shard_map/ppermute | solution.py:435
  3.8 0.7 %copy-start = (s32[1,1,2,64]{3,2,1,0:T(2,128)S(1)}, s32[1,1,2,64]{3,2,1,0:T(2,128)}, u32[]{:S(2)}) copy-start(s32[1,1,2,64]{3,2,1,0:T(2,128)} %param.9) | copy-start | bytes 1540
  5.3 13.3 %all-to-all-start = ((s32[32,1,8]{2,1,0:T(1,128)}), s32[32,1,8]{2,1,0:T(1,128)S(1)}, u32[]{:S(2)}, u32[]{:S(2)}) async-start(s32[32,1,8]{2,1,0:T(1,128)} %bitcast.3), calls=%async_computation | async-start | bytes 32768 | tf_op jit(solution)/shard_map/all_to_all | solution.py:431
